TPU v7x, 128 devices: a whole 4x4x4 slice. The times are simulated.
128 devices in a mesh: ctx: 64 (over x_lo, z, y, core), fsdp: 2 (over x_hi).
Axes of the slice: x: 4 (x_hi: 2, x_lo: 2; x = x_hi * 2 + x_lo), y: 4, z: 4, core: 2. Of those that a mesh axis runs over, the one named last changes fastest.
Arguments:
- inputs: bfloat16 [2, 8192, 640], P('fsdp', 'ctx'), may hold values from -6 to 6
- pair_order: int32 [64], replicated, may hold values from 0 to 63, each once
- w_query: bfloat16 [640, 1024], P('fsdp'), may hold values from -0.25 to 0.25
- w_key: bfloat16 [640, 256], P('fsdp'), may hold values from -0.25 to 0.25
- w_value: bfloat16 [640, 256], P('fsdp'), may hold values from -0.25 to 0.25
- w_output: bfloat16 [1024, 640], P('fsdp'), may hold values from -0.1875 to 0.1875
- w_gate: bfloat16 [640, 2048], P('fsdp'), may hold values from -0.25 to 0.25
- w_up: bfloat16 [640, 2048], P('fsdp'), may hold values from -0.25 to 0.25
- w_down: bfloat16 [2048, 640], P('fsdp'), may hold values from -0.125 to 0.125
- gain_in: float32 [640], replicated, may hold values from 0.25 to 1.75
- gain_query: float32 [256], replicated, may hold values from 0.25 to 1.75
- gain_key: float32 [256], replicated, may hold values from 0.25 to 1.75
- gain_post_attn: float32 [640], replicated, may hold values from 0.25 to 1.75
- gain_pre_ff: float32 [640], replicated, may hold values from 0.25 to 1.75
- gain_post_ff: float32 [640], replicated, may hold values from 0.25 to 1.75
- cotangent: bfloat16 [2, 8192, 640], P('fsdp', 'ctx'), may hold values from -6 to 6
Outputs:
- layer_out: bfloat16 [2, 8192, 640], P('fsdp', 'ctx')
- input_grad: bfloat16 [2, 8192, 640], P('fsdp', 'ctx')
- grad_query: float32 [640, 1024], P(('ctx', 'fsdp'))
- grad_key: float32 [640, 256], P(('ctx', 'fsdp'))
- grad_value: float32 [640, 256], P(('ctx', 'fsdp'))
- grad_output: float32 [1024, 640], P(('ctx', 'fsdp'))
- grad_gate: float32 [640, 2048], P(('ctx', 'fsdp'))
- grad_up: float32 [640, 2048], P(('ctx', 'fsdp'))
- grad_down: float32 [2048, 640], P(('ctx', 'fsdp'))
- grad_gain_in: float32 [640], P(('ctx', 'fsdp'))
- grad_gain_query: float32 [256], P(('ctx', 'fsdp'))
- grad_gain_key: float32 [256], P(('ctx', 'fsdp'))
- grad_gain_post_attn: float32 [640], P(('ctx', 'fsdp'))
- grad_gain_pre_ff: float32 [640], P(('ctx', 'fsdp'))
- grad_gain_post_ff: float32 [640], P(('ctx', 'fsdp'))
Inputs may be any that keep to these rules, and one draw needn't show every extreme that they name: Index i of ctx holds blocks pair_order[i] and 127 - pair_order[i] of every sequence, 64 tokens each, in that order; every pair is held once.
All inputs are finite; a program needn't handle non-finite values.
Results may differ from a plain program's by a relative error of at most 0.038.
Values may be sent and summed in bfloat16 or wider, within the bound.
A program may use at most 128 MiB of HBM per device.

v0:
```python
import math

import jax
import jax.numpy as jnp
from jax import lax
from jax.sharding import PartitionSpec as P

EPS = 1e-06
ROPE_BASE = 1000000.0
SCALE = 0.0625
MASKED = -1e30


def norm_scale(values, gain):
    return values * lax.rsqrt(jnp.mean(values * values, axis=-1, keepdims=True) + EPS) * gain


def rotate(values, angles):
    half = values.shape[-1] // 2
    first = values[..., :half]
    second = values[..., half:]
    cosine = jnp.cos(angles)
    sine = jnp.sin(angles)
    return jnp.concatenate(
        [first * cosine - second * sine, second * cosine + first * sine], axis=-1
    )


def row_positions(pair_order, first_row, count, block_len, ndev):
    rows = first_row + jnp.arange(count, dtype=jnp.int32)
    device = rows // (2 * block_len)
    within = rows % (2 * block_len)
    pair = jnp.take(pair_order, device)
    block_id = jnp.where(within < block_len, pair, 2 * ndev - 1 - pair)
    return block_id * block_len + within % block_len


def to_position_order(gathered, inverse, ndev, block_len):
    grouped = gathered.reshape(ndev, 2, block_len, gathered.shape[-1])
    early = jnp.take(grouped[:, 0], inverse, axis=0)
    late = jnp.take(grouped[:, 1], inverse, axis=0)[::-1]
    return jnp.concatenate([early, late], axis=0).reshape(2 * ndev * block_len, gathered.shape[-1])


def to_device_order(ordered, pair_order, ndev, block_len):
    grouped = ordered.reshape(2 * ndev, block_len, ordered.shape[-1])
    early = jnp.take(grouped[:ndev], pair_order, axis=0)
    late = jnp.take(grouped[ndev:][::-1], pair_order, axis=0)
    return jnp.stack([early, late], axis=1).reshape(2 * ndev * block_len, ordered.shape[-1])


def local(
    inputs,
    pair_order,
    w_query,
    w_key,
    w_value,
    w_output,
    w_gate,
    w_up,
    w_down,
    gain_in,
    gain_query,
    gain_key,
    gain_post_attn,
    gain_pre_ff,
    gain_post_ff,
    cotangent,
):
    f32 = jnp.float32
    bf16 = jnp.bfloat16
    ndev = lax.axis_size("ctx")
    rows = inputs.shape[1]
    block_len = rows // 2
    total = rows * ndev
    head_dim = gain_query.shape[0]
    heads = w_query.shape[1] // head_dim
    me_index = lax.axis_index("ctx")
    positions = row_positions(pair_order, me_index * rows, rows, block_len, ndev)
    half = head_dim // 2
    freq = ROPE_BASE ** (-jnp.arange(half, dtype=f32) / half)
    angles = positions.astype(f32)[:, None] * freq
    matches = pair_order[None, :] == jnp.arange(ndev, dtype=jnp.int32)[:, None]
    inverse = jnp.sum(jnp.where(matches, jnp.arange(ndev, dtype=jnp.int32)[None, :], 0), axis=1)
    own_pair = jnp.take(pair_order, me_index)
    block_ids = (own_pair, 2 * ndev - 1 - own_pair)

    def prepare(query_lin, key_lin, g_query, g_key):
        query = rotate(
            norm_scale(query_lin.reshape(rows, heads, head_dim), g_query), angles[:, None, :]
        )
        key = rotate(norm_scale(key_lin, g_key), angles)
        return (query, key)

    weights = (
        lax.all_gather(w_query, "fsdp", axis=0, tiled=True),
        lax.all_gather(w_key, "fsdp", axis=0, tiled=True),
        lax.all_gather(w_value, "fsdp", axis=0, tiled=True),
        lax.all_gather(w_output, "fsdp", axis=0, tiled=True),
        lax.all_gather(w_gate, "fsdp", axis=0, tiled=True),
        lax.all_gather(w_up, "fsdp", axis=0, tiled=True),
        lax.all_gather(w_down, "fsdp", axis=0, tiled=True),
    )
    wq_all, wk_all, wv_all, wo_all, wg_all, wu_all, wd_all = weights
    states = inputs[0].astype(f32)
    act_one = norm_scale(states, gain_in).astype(bf16)
    query_lin = jnp.dot(act_one, wq_all, preferred_element_type=f32)
    key_lin = jnp.dot(act_one, wk_all, preferred_element_type=f32)
    value_b = jnp.dot(act_one, wv_all, preferred_element_type=f32).astype(bf16)
    query_rot, key_rot = prepare(query_lin, key_lin, gain_query, gain_key)
    query_b = query_rot.astype(bf16).reshape(rows * heads, head_dim)
    key_b = key_rot.astype(bf16)
    query_pos = jnp.repeat(positions, heads)
    qrows = rows * heads
    part_rows = block_len * heads
    query_parts = (query_b[:part_rows], query_b[part_rows:])
    qpos_parts = (query_pos[:part_rows], query_pos[part_rows:])
    kblock = math.gcd(512, total)
    key_all, value_all = (
        lax.all_gather(key_b, "ctx", axis=0, tiled=True),
        lax.all_gather(value_b, "ctx", axis=0, tiled=True),
    )
    key_sorted = to_position_order(key_all, inverse, ndev, block_len)
    value_sorted = to_position_order(value_all, inverse, ndev, block_len)

    def key_steps(block_id):
        return ((block_id + 1) * block_len + kblock - 1) // kblock

    def scores_for(qpart, qpos, keys_sorted, step):
        keys_piece = lax.dynamic_slice_in_dim(keys_sorted, step * kblock, kblock, 0)
        key_pos = step * kblock + jnp.arange(kblock, dtype=jnp.int32)
        raw = jnp.einsum("qd,kd->qk", qpart, keys_piece, preferred_element_type=f32) * SCALE
        visible = key_pos[None, :] <= qpos[:, None]
        return (raw, visible, keys_piece)

    log_parts = []
    attended_parts = []
    for part in range(2):
        qpart = query_parts[part]
        qpos = qpos_parts[part]
        steps_needed = key_steps(block_ids[part])

        def stats_step(step, carry):
            top, weight_sum = carry
            raw, visible, unused = scores_for(qpart, qpos, key_sorted, step)
            raw = jnp.where(visible, raw, MASKED)
            new_top = jnp.maximum(top, jnp.max(raw, axis=1))
            weight_sum = weight_sum * jnp.exp(top - new_top) + jnp.sum(
                jnp.exp(raw - new_top[:, None]), axis=1
            )
            return (new_top, weight_sum)

        top, weight_sum = lax.fori_loop(
            0,
            steps_needed,
            stats_step,
            (jnp.full((part_rows,), MASKED, f32), jnp.zeros((part_rows,), f32)),
        )
        log_total = top + jnp.log(weight_sum)

        def value_step(step, accum):
            raw, visible, unused = scores_for(qpart, qpos, key_sorted, step)
            probs_b = jnp.where(visible, jnp.exp(raw - log_total[:, None]), 0.0).astype(bf16)
            values_piece = lax.dynamic_slice_in_dim(value_sorted, step * kblock, kblock, 0)
            return accum + jnp.dot(probs_b, values_piece, preferred_element_type=f32)

        attended_parts.append(
            lax.fori_loop(0, steps_needed, value_step, jnp.zeros((part_rows, head_dim), f32))
        )
        log_parts.append(log_total)
    attended = jnp.concatenate(attended_parts, axis=0)
    attended_b = attended.astype(bf16)
    attended_flat = attended_b.reshape(rows, heads * head_dim)
    att_lin = jnp.dot(attended_flat, wo_all, preferred_element_type=f32)
    resid = states + norm_scale(att_lin, gain_post_attn)
    act_two = norm_scale(resid, gain_pre_ff).astype(bf16)
    gate = jnp.dot(act_two, wg_all, preferred_element_type=f32)
    upper = jnp.dot(act_two, wu_all, preferred_element_type=f32)
    hidden_b = (jax.nn.gelu(gate, approximate=True) * upper).astype(bf16)
    down = jnp.dot(hidden_b, wd_all, preferred_element_type=f32)
    layer_out = resid + norm_scale(down, gain_post_ff)
    back_weights = (
        lax.all_gather(w_query, "fsdp", axis=0, tiled=True),
        lax.all_gather(w_key, "fsdp", axis=0, tiled=True),
        lax.all_gather(w_value, "fsdp", axis=0, tiled=True),
        lax.all_gather(w_output, "fsdp", axis=0, tiled=True),
        lax.all_gather(w_gate, "fsdp", axis=0, tiled=True),
        lax.all_gather(w_up, "fsdp", axis=0, tiled=True),
        lax.all_gather(w_down, "fsdp", axis=0, tiled=True),
    )
    wq_all, wk_all, wv_all, wo_all, wg_all, wu_all, wd_all = back_weights
    grad_y = cotangent[0].astype(f32)
    unused_out, post_ff_back = jax.vjp(norm_scale, down, gain_post_ff)
    d_down, d_gain_post_ff = post_ff_back(grad_y)
    d_down_b = d_down.astype(bf16)
    grad_down = jnp.einsum("rf,rd->fd", hidden_b, d_down_b, preferred_element_type=f32)
    d_hidden = jnp.einsum("rd,fd->rf", d_down_b, wd_all, preferred_element_type=f32)
    unused_act, act_back = jax.vjp(
        lambda gate_in, up_in: jax.nn.gelu(gate_in, approximate=True) * up_in, gate, upper
    )
    d_gate, d_upper = act_back(d_hidden)
    d_gate_b = d_gate.astype(bf16)
    d_upper_b = d_upper.astype(bf16)
    grad_gate = jnp.einsum("rd,rf->df", act_two, d_gate_b, preferred_element_type=f32)
    grad_up = jnp.einsum("rd,rf->df", act_two, d_upper_b, preferred_element_type=f32)
    d_act_two = jnp.einsum("rf,df->rd", d_gate_b, wg_all, preferred_element_type=f32) + jnp.einsum(
        "rf,df->rd", d_upper_b, wu_all, preferred_element_type=f32
    )
    unused_two, pre_ff_back = jax.vjp(norm_scale, resid, gain_pre_ff)
    d_resid_part, d_gain_pre_ff = pre_ff_back(d_act_two)
    grad_resid = grad_y + d_resid_part
    unused_three, post_attn_back = jax.vjp(norm_scale, att_lin, gain_post_attn)
    d_att, d_gain_post_attn = post_attn_back(grad_resid)
    d_att_b = d_att.astype(bf16)
    grad_output = jnp.einsum("re,rd->ed", attended_flat, d_att_b, preferred_element_type=f32)
    d_attended_b = (
        jnp.einsum("rd,ed->re", d_att_b, wo_all, preferred_element_type=f32)
        .astype(bf16)
        .reshape(qrows, head_dim)
    )
    row_delta = jnp.sum(d_attended_b.astype(f32) * attended, axis=1)
    key_back, value_back = (
        lax.all_gather(key_b, "ctx", axis=0, tiled=True),
        lax.all_gather(value_b, "ctx", axis=0, tiled=True),
    )
    key_back_sorted = to_position_order(key_back, inverse, ndev, block_len)
    value_back_sorted = to_position_order(value_back, inverse, ndev, block_len)
    d_key_sorted = jnp.zeros((total, head_dim), f32)
    d_value_sorted = jnp.zeros((total, head_dim), f32)
    dq_parts = []
    for part in range(2):
        qpart = query_parts[part]
        qpos = qpos_parts[part]
        log_total = log_parts[part]
        dattn_part = d_attended_b[part * part_rows : (part + 1) * part_rows]
        delta_part = row_delta[part * part_rows : (part + 1) * part_rows]

        def backward_step(step, carry):
            dq_total, dk_total, dv_total = carry
            raw, visible, keys_piece = scores_for(qpart, qpos, key_back_sorted, step)
            values_piece = lax.dynamic_slice_in_dim(value_back_sorted, step * kblock, kblock, 0)
            probs = jnp.where(visible, jnp.exp(raw - log_total[:, None]), 0.0)
            d_probs = jnp.einsum("qd,kd->qk", dattn_part, values_piece, preferred_element_type=f32)
            d_scores = (probs * (d_probs - delta_part[:, None])).astype(bf16)
            probs_b = probs.astype(bf16)
            dq_total = dq_total + jnp.dot(d_scores, keys_piece, preferred_element_type=f32)
            d_key_piece = jnp.einsum("qk,qd->kd", d_scores, qpart, preferred_element_type=f32)
            d_value_piece = jnp.einsum("qk,qd->kd", probs_b, dattn_part, preferred_element_type=f32)
            dk_total = lax.dynamic_update_slice_in_dim(
                dk_total,
                lax.dynamic_slice_in_dim(dk_total, step * kblock, kblock, 0) + d_key_piece,
                step * kblock,
                0,
            )
            dv_total = lax.dynamic_update_slice_in_dim(
                dv_total,
                lax.dynamic_slice_in_dim(dv_total, step * kblock, kblock, 0) + d_value_piece,
                step * kblock,
                0,
            )
            return (dq_total, dk_total, dv_total)

        dq_part, d_key_sorted, d_value_sorted = lax.fori_loop(
            0,
            key_steps(block_ids[part]),
            backward_step,
            (jnp.zeros((part_rows, head_dim), f32), d_key_sorted, d_value_sorted),
        )
        dq_parts.append(dq_part)
    dq_total = jnp.concatenate(dq_parts, axis=0)
    d_key_all = to_device_order(d_key_sorted * SCALE, pair_order, ndev, block_len)
    d_value_all = to_device_order(d_value_sorted, pair_order, ndev, block_len)
    d_key_own, d_value_own = (
        lax.psum_scatter(d_key_all, "ctx", scatter_dimension=0, tiled=True),
        lax.psum_scatter(d_value_all, "ctx", scatter_dimension=0, tiled=True),
    )
    d_value_b = d_value_own.astype(bf16)
    d_query = (dq_total * SCALE).reshape(rows, heads, head_dim)
    unused_four, prep_back = jax.vjp(prepare, query_lin, key_lin, gain_query, gain_key)
    d_query_lin, d_key_lin, d_gain_query, d_gain_key = prep_back((d_query, d_key_own))
    d_query_lin_b = d_query_lin.astype(bf16)
    d_key_lin_b = d_key_lin.astype(bf16)
    grad_query = jnp.einsum("rd,re->de", act_one, d_query_lin_b, preferred_element_type=f32)
    grad_key = jnp.einsum("rd,re->de", act_one, d_key_lin_b, preferred_element_type=f32)
    grad_value = jnp.einsum("rd,re->de", act_one, d_value_b, preferred_element_type=f32)
    d_act_one = jnp.einsum("re,de->rd", d_query_lin_b, wq_all, preferred_element_type=f32)
    d_act_one = d_act_one + jnp.einsum("re,de->rd", d_key_lin_b, wk_all, preferred_element_type=f32)
    d_act_one = d_act_one + jnp.einsum("re,de->rd", d_value_b, wv_all, preferred_element_type=f32)
    unused_five, pre_attn_back = jax.vjp(norm_scale, states, gain_in)
    d_states, d_gain_in = pre_attn_back(d_act_one)
    input_grad = grad_resid + d_states
    summed = (
        lax.psum_scatter(grad_query, ("ctx", "fsdp"), scatter_dimension=0, tiled=True),
        lax.psum_scatter(grad_key, ("ctx", "fsdp"), scatter_dimension=0, tiled=True),
        lax.psum_scatter(grad_value, ("ctx", "fsdp"), scatter_dimension=0, tiled=True),
        lax.psum_scatter(grad_output, ("ctx", "fsdp"), scatter_dimension=0, tiled=True),
        lax.psum_scatter(grad_gate, ("ctx", "fsdp"), scatter_dimension=0, tiled=True),
        lax.psum_scatter(grad_up, ("ctx", "fsdp"), scatter_dimension=0, tiled=True),
        lax.psum_scatter(grad_down, ("ctx", "fsdp"), scatter_dimension=0, tiled=True),
        lax.psum_scatter(d_gain_in, ("ctx", "fsdp"), scatter_dimension=0, tiled=True),
        lax.psum_scatter(d_gain_query, ("ctx", "fsdp"), scatter_dimension=0, tiled=True),
        lax.psum_scatter(d_gain_key, ("ctx", "fsdp"), scatter_dimension=0, tiled=True),
        lax.psum_scatter(d_gain_post_attn, ("ctx", "fsdp"), scatter_dimension=0, tiled=True),
        lax.psum_scatter(d_gain_pre_ff, ("ctx", "fsdp"), scatter_dimension=0, tiled=True),
        lax.psum_scatter(d_gain_post_ff, ("ctx", "fsdp"), scatter_dimension=0, tiled=True),
    )
    return (
        layer_out.astype(bf16)[None],
        input_grad.astype(bf16)[None],
        summed[0],
        summed[1],
        summed[2],
        summed[3],
        summed[4],
        summed[5],
        summed[6],
        summed[7],
        summed[8],
        summed[9],
        summed[10],
        summed[11],
        summed[12],
    )


def solution(mesh):
    placed = (
        P("fsdp", "ctx", None),
        P(),
        P("fsdp", None),
        P("fsdp", None),
        P("fsdp", None),
        P("fsdp", None),
        P("fsdp", None),
        P("fsdp", None),
        P("fsdp", None),
        P(),
        P(),
        P(),
        P(),
        P(),
        P(),
        P("fsdp", "ctx", None),
    )
    return jax.shard_map(
        local,
        mesh=mesh,
        in_specs=placed,
        out_specs=(
            P("fsdp", "ctx", None),
            P("fsdp", "ctx", None),
            P(("ctx", "fsdp"), None),
            P(("ctx", "fsdp"), None),
            P(("ctx", "fsdp"), None),
            P(("ctx", "fsdp"), None),
            P(("ctx", "fsdp"), None),
            P(("ctx", "fsdp"), None),
            P(("ctx", "fsdp"), None),
            P(("ctx", "fsdp")),
            P(("ctx", "fsdp")),
            P(("ctx", "fsdp")),
            P(("ctx", "fsdp")),
            P(("ctx", "fsdp")),
            P(("ctx", "fsdp")),
        ),
        check_vma=False,
    )
```

profile of v0, /device:TPU:0, one launch (start us, length us, event | category | flops | bytes accessed | tf_op | source)
XLA Modules:
  0.0 2111.9 jit_solution(16286180904147295692)
XLA Ops:
  11.2 8.2 all_gather.36
  24.0 12.4 all_gather.39
  46.9 104.8 %all-gather.8.cloned.1.call-done = bf16[8192,256]{1,0:T(8,128)(2,1)} async-done(((bf16[128,256]{1,0:T(8,128)(2,1)}), bf16[8192,256]{1,0:T(8,128)(2,1)}) %all-gather.8.cloned.1.call-update) | async-done | bytes 4194320 | tf_op jit(solution)/shard_map/all_gather | solution.py:120
  151.7 4.0 slice_bitcast_fusion.3
  155.8 3.7 gather_fusion.2
  161.5 97.6 %all-gather.12.cloned.1.call-done = bf16[8192,256]{1,0:T(8,128)(2,1)} async-done(((bf16[128,256]{1,0:T(8,128)(2,1)}), bf16[8192,256]{1,0:T(8,128)(2,1)}) %all-gather.12.cloned.1.call-update) | async-done | bytes 4194320 | tf_op jit(solution)/shard_map/all_gather | solution.py:121
  259.0 4.0 slice_bitcast_fusion.1
  263.1 3.6 gather_fusion.3
  268.7 6.2 broadcast_select_fusion.1
  274.8 3.2 rev.14
  278.0 4.6 pad_maximum_fusion.2
  282.6 14.7 while.81
  298.8 4.9 pad_maximum_fusion.3
  303.7 16.4 while.82
  320.2 13.1 while.79
  333.3 15.0 while.80
  350.9 2.3 fusion.170
  353.2 22.7 %all-gather.18.cloned.1.call-done = bf16[640,2048]{1,0:T(8,128)(2,1)} async-done(((bf16[320,2048]{1,0:T(8,128)(2,1)}), bf16[640,2048]{1,0:T(8,128)(2,1)}) %all-gather.18.cloned.1.call-update) | async-done | bytes 2621456 | tf_op jit(solution)/shard_map/all_gather | solution.py:101
  375.9 3.5 multiply_convert_fusion.1
  379.5 40.6 %all-gather.20.cloned.1.call-done = bf16[2048,640]{1,0:T(8,128)(2,1)} async-done(((bf16[1024,640]{1,0:T(8,128)(2,1)}), bf16[2048,640]{1,0:T(8,128)(2,1)}) %all-gather.20.cloned.1.call-update) | async-done | bytes 2621456 | tf_op jit(solution)/shard_map/all_gather | solution.py:102
  420.0 2.6 multiply_reduce_fusion.8
  433.4 3.8 broadcast.558
  437.2 3.7 broadcast.558.clone
  441.0 64.8 %while.83 = (s32[]{:T(128)}, f32[256,256]{1,0:T(8,128)S(1)}, f32[8192,256]{1,0:T(8,128)}, f32[8192,256]{1,0:T(8,128)}, s32[]{:T(128)}, /*index=5*/bf16[8192,256]...) while((s32[]{:T(128)}, f32[256,256]{1,0:T(8,128)S(1)}, ...), condition=%wide.region_24.26_spmd.clone, body=%wide.region_23.25_spmd.clone.sunk | while | flops 336921088 | bytes 6302171 | solution.py:263
  505.9 73.2 %while.84 = (s32[]{:T(128)}, f32[256,256]{1,0:T(8,128)S(1)}, f32[8192,256]{1,0:T(8,128)}, f32[8192,256]{1,0:T(8,128)}, s32[]{:T(128)}, /*index=5*/bf16[8192,256]...) while((s32[]{:T(128)}, f32[256,256]{1,0:T(8,128)S(1)}, ...), condition=%wide.region_26.28_spmd.clone, body=%wide.region_25.27_spmd.clone.sunk | while | flops 336921088 | bytes 6302171 | solution.py:263
  573.5 2.1 fusion.301
  579.1 3.9 broadcast_multiply_fusion
  583.1 3.9 fusion.165
  587.0 4.7 rev.16
  591.7 5.0 gather_fusion.6
  596.7 5.0 gather_fusion.5
  601.7 7.2 fusion.164
  608.9 4.6 rev.17
  613.5 4.9 gather_fusion.8
  618.5 5.0 gather_fusion.7
  623.4 9.2 select_bitcast_fusion.1
  632.7 3.9 pad_maximum_fusion
  636.6 7.9 pad_maximum_fusion.1
  646.1 3.0 fusion.173
  649.1 2.1 fusion.121
  651.3 3.2 fusion.174
  654.5 3.1 fusion.175
  657.6 276.6 %reduce-scatter.4.cloned.1.call-done = f32[128,256]{1,0:T(8,128)} async-done(((f32[8192,256]{1,0:T(8,128)}), f32[128,256]{1,0:T(8,128)}) %reduce-scatter.4.cloned.1.call-update) | async-done | bytes 131088 | tf_op jit(solution)/shard_map/reduce_scatter | solution.py:274
  936.9 294.6 %reduce-scatter.6.cloned.1.call-done = f32[128,256]{1,0:T(8,128)} async-done(((f32[8192,256]{1,0:T(8,128)}), f32[128,256]{1,0:T(8,128)}) %reduce-scatter.6.cloned.1.call-update) | async-done | bytes 131088 | tf_op jit(solution)/shard_map/reduce_scatter | solution.py:275
  1234.6 3.2 fusion.176
  1240.3 64.5 %all-reduce.16 = (f32[640]{0:T(1024)S(1)}, f32[256]{0:T(256)S(1)}, f32[256]{0:T(256)S(1)}, f32[640]{0:T(1024)S(1)}, f32[640]{0:T(1024)S(1)}, /*index=5*/f32[640]{0:T(1024)S(1)}) all-reduce(f32[640]{0:T(1024)S(1)} %get-tuple-element.474, f32[256]{0:T(256)S(1)} %get-tuple-element.466, ...), channel_id=11, replica_groups=mesh['ctx'=64,'fsdp'=2] {'ctx','fsdp'}, use_global_device_ids=true, to_apply=%region_40.43.clone | all-reduce | flops 3072 | bytes 24576
  1309.1 147.8 %all-reduce.20.cloned.1.call-done = (f32[640,1024]{1,0:T(8,128)}, f32[640,256]{1,0:T(8,128)}, f32[640,256]{1,0:T(8,128)}, f32[1024,640]{1,0:T(8,128)}, f32[640,2048]{1,0:T(8,128)}, /*index=5*/f32[640,2048]{1,0:T(8,128)}) async-done(((f32[640,1024]{1,0:T(8,128)}, f32[640,256]{1,0:T(8,128)}, f32[640,256]{1,0:T(8,128)}, f32[1024,640]{1,0:T(8,128)}, f32[640,2048]{1,0:T(8,128)}, ...) | async-done | bytes 17039376
  1465.5 639.9 %reduce-scatter.8.cloned.1.call-done = f32[16,640]{1,0:T(8,128)} async-done(((f32[2048,640]{1,0:T(8,128)}), f32[16,640]{1,0:T(8,128)}) %reduce-scatter.8.cloned.1.call-update) | async-done | bytes 40976 | tf_op jit(solution)/shard_map/reduce_scatter | solution.py:299
  (564 shorter events, 251.7 us)
Async XLA Ops:
  7.2 36.8 %all-gather.10.cloned.1.call-start = ((), (), s32[]{:S(2)}) async-start(), calls=%async_computation.4 | async-start | bytes 1966080 | tf_op jit(solution)/shard_map/all_gather | solution.py:96
  7.9 32.9 %copy-start = (s32[64]{0:T(128)S(1)}, s32[64]{0:T(128)}, u32[]{:S(2)}) copy-start(s32[64]{0:T(128)} %param.33) | copy-start | bytes 772
  7.9 143.8 %all-gather.8.cloned.1.call-start = ((), (), s32[]{:S(2)}) async-start(), calls=%async_computation.3 | async-start | bytes 4259840 | tf_op jit(solution)/shard_map/all_gather | solution.py:120
  8.0 34.2 %copy-start.42 = (f32[128]{0:T(128)}, f32[128]{0:T(128)S(1)}, u32[]{:S(2)}) copy-start(f32[128]{0:T(128)S(1)} %multiply_power_fusion) | copy-start | bytes 1540
  23.2 23.3 %copy-start.31 = (f32[128,128]{1,0:T(8,128)}, f32[128,128]{1,0:T(8,128)S(1)}, u32[]{:S(2)}) copy-start(f32[128,128]{1,0:T(8,128)S(1)} %get-tuple-element.636) | copy-start | bytes 196612
  23.9 21.8 %copy-start.3 = (bf16[1,128,640]{2,1,0:T(8,128)(2,1)S(1)}, bf16[1,128,640]{2,1,0:T(8,128)(2,1)}, u32[]{:S(2)}) copy-start(bf16[1,128,640]{2,1,0:T(8,128)(2,1)} %param.32) | copy-start | bytes 491524
  23.9 21.8 %copy-start.34 = (f32[640]{0:T(1024)S(1)}, f32[640]{0:T(1024)}, u32[]{:S(2)}) copy-start(f32[640]{0:T(1024)} %param.41) | copy-start | bytes 7684
  23.9 235.1 %all-gather.12.cloned.1.call-start = ((), (), s32[]{:S(2)}) async-start(), calls=%async_computation.5 | async-start | bytes 4259840 | tf_op jit(solution)/shard_map/all_gather | solution.py:121
  36.3 10.0 copy-start.24
  38.3 310.3 %all-gather.14.cloned.1.call-start = ((), (), s32[]{:S(2)}) async-start(), calls=%async_computation.6 | async-start | bytes 1966080 | tf_op jit(solution)/shard_map/all_gather | solution.py:99
  38.9 7.5 copy-start.39
  38.9 312.0 %all-gather.16.cloned.1.call-start = ((), (), s32[]{:S(2)}) async-start(), calls=%async_computation.7 | async-start | bytes 3932160 | tf_op jit(solution)/shard_map/all_gather | solution.py:100
  39.5 336.5 %all-gather.18.cloned.1.call-start = ((), (), s32[]{:S(2)}) async-start(), calls=%async_computation.8 | async-start | bytes 3932160 | tf_op jit(solution)/shard_map/all_gather | solution.py:101
  40.0 380.0 %all-gather.20.cloned.1.call-start = ((), (), s32[]{:S(2)}) async-start(), calls=%async_computation.9 | async-start | bytes 3932160 | tf_op jit(solution)/shard_map/all_gather | solution.py:102
  40.8 893.4 %reduce-scatter.4.cloned.1.call-start = ((), (), s32[]{:S(2)}) async-start(), calls=%async_computation.10 | async-start | bytes 8519680 | tf_op jit(solution)/shard_map/reduce_scatter | solution.py:274
  320.2 13.1 copy-start.6
  348.3 2.2 copy-start.8
  348.3 2.2 copy-start.36
  348.3 2.4 copy-start.35
  348.4 4.8 copy-start.10
  348.6 2.1 copy-start.14
  353.2 69.4 %copy-start.37 = (f32[640]{0:T(1024)S(1)}, f32[640]{0:T(1024)}, u32[]{:S(2)}) copy-start(f32[640]{0:T(1024)} %param.46) | copy-start | bytes 7684
  420.0 5.4 copy-start.13
  420.0 5.4 copy-start.28
  425.5 1.8 copy-start.1
  425.5 3.0 copy-start.2
  426.9 3.0 copy-start.16
  426.9 2.9 copy-start.18
  426.9 2.6 copy-start.21
  427.3 4.1 copy-start.5
  437.2 3.8 copy-start.9
  441.0 65.0 %copy-start.7 = (bf16[256,256]{1,0:T(8,128)(2,1)S(1)}, bf16[256,256]{1,0:T(8,128)(2,1)}, u32[]{:S(2)}) copy-start(bf16[256,256]{1,0:T(8,128)(2,1)} %copy-done.6) | copy-start | bytes 393220
  618.5 5.0 copy-start.46
  636.6 595.0 %reduce-scatter.6.cloned.1.call-start = ((), (), s32[]{:S(2)}) async-start(), calls=%async_computation.11 | async-start | bytes 8519680 | tf_op jit(solution)/shard_map/reduce_scatter | solution.py:275
  644.6 812.4 %all-reduce.20.cloned.1.call-start = ((), (), s32[]{:S(2)}) async-start(), calls=%async_computation.13 | async-start | bytes 34078720
  645.7 5.6 copy-start.19
  651.3 3.2 copy-start.17
  654.5 279.8 %copy-start.41 = (f32[128]{0:T(128)S(1)}, f32[128]{0:T(128)}, u32[]{:S(2)}) copy-start(f32[128]{0:T(128)} %copy-done.40) | copy-start | bytes 1540
  654.5 279.8 %copy-start.43 = (f32[128]{0:T(128)S(1)}, f32[128]{0:T(128)}, u32[]{:S(2)}) copy-start(f32[128]{0:T(128)} %copy-done.42) | copy-start | bytes 1540
  654.5 281.0 %copy-start.27 = (f32[128,256]{1,0:T(8,128)S(1)}, f32[128,256]{1,0:T(8,128)}, u32[]{:S(2)}) copy-start(f32[128,256]{1,0:T(8,128)} %copy-done.26) | copy-start | bytes 393220
  654.5 281.0 %copy-start.38 = (f32[256]{0:T(256)S(1)}, f32[256]{0:T(256)}, u32[]{:S(2)}) copy-start(f32[256]{0:T(256)} %param.43) | copy-start | bytes 3076
  654.5 281.1 %copy-start.48 = (f32[128]{0:T(128)S(1)}, f32[128]{0:T(128)}, u32[]{:S(2)}) copy-start(f32[128]{0:T(128)} %copy-done.47) | copy-start | bytes 1540
  1233.7 871.7 %reduce-scatter.8.cloned.1.call-start = ((), (), s32[]{:S(2)}) async-start(), calls=%async_computation.12 | async-start | bytes 5283840 | tf_op jit(solution)/shard_map/reduce_scatter | solution.py:299
  1237.8 1.9 copy-start.23
  1237.8 2.1 copy-start.25
  1237.8 2.1 copy-start.33
  1237.8 70.5 %copy-start.45 = (f32[128]{0:T(128)S(1)}, f32[128]{0:T(128)}, u32[]{:S(2)}) copy-start(f32[128]{0:T(128)} %copy-done.44) | copy-start | bytes 1540
  1237.8 70.5 %copy-start.12 = (f32[128,640]{1,0:T(8,128)S(1)}, f32[128,640]{1,0:T(8,128)}, u32[]{:S(2)}) copy-start(f32[128,640]{1,0:T(8,128)} %copy-done.11) | copy-start | bytes 983044
  (12 other events, 11.8 us)
Sparse Core Ops, SparseCore 0:
  9.7 34.2 all-gather.9
  46.2 105.4 all-gather.7
  154.0 104.9 all-gather.11
  260.5 27.2 all-gather.13
  289.3 42.4 all-gather.15
  333.3 42.5 all-gather.17
  377.6 42.3 all-gather.19
  636.7 297.4 reduce-scatter.3
  936.6 294.8 reduce-scatter.5
  1237.8 219.0 all-reduce.19
  1459.9 645.4 reduce-scatter.7
where the time goes:
time: 2120 us; the launch traced here: 2110 us
  waiting for transfers between devices  1630 us (77%)
  matrix products  220 us (10%)
  local copies, waits for them, and re-layouts  105 us (5%)
  blocking collectives  85.1 us (4%)
  other arithmetic  54.6 us (3%)
    reduce_scatter x1, waiting for transfers between devices, local(): lax.psum_scatter(grad_down, ('ctx', 'fsdp'), scatter_dimension=0, tiled=T...  640 us
    reduce_scatter x1, waiting for transfers between devices, local(): lax.psum_scatter(d_value_all, 'ctx', scatter_dimension=0, tiled=True)  295 us
    reduce_scatter x1, waiting for transfers between devices, local(): lax.psum_scatter(d_key_all, 'ctx', scatter_dimension=0, tiled=True)  277 us
    unnamed x12, waiting for transfers between devices  151 us
    all_gather x1, waiting for transfers between devices, local(): lax.all_gather(key_b, 'ctx', axis=0, tiled=True)  105 us
    all_gather x1, waiting for transfers between devices, local(): lax.all_gather(value_b, 'ctx', axis=0, tiled=True)  97.6 us
    unnamed x1, blocking collectives  64.5 us
    dot_general x34, matrix products, scores_for(): jnp.einsum('qd,kd->qk', qpart, keys_piece, preferred_element_type=f32)  42.6 us
  transfers between devices with their start and end apart: 11, of which 9 were waited for; matrix products, arithmetic and copies ran while one was open for 7% of the time, Pallas kernels for 0%

commit v1 on v0

v1 whole, which is shorter than its diff:
```python
import functools
import math

import jax
import jax.numpy as jnp
from jax import lax
from jax.experimental import pallas as pl
from jax.experimental.pallas import tpu as pltpu
from jax.sharding import PartitionSpec as P

EPS = 1e-06
ROPE_BASE = 1000000.0
SCALE = 0.0625
EXP2_SCALE = SCALE * math.log2(math.e)
MESH = pl.DeviceIdType.MESH
BF16 = jnp.bfloat16
F32 = jnp.float32
ANY = pl.BlockSpec(memory_space=pl.ANY)
VMEM = pl.BlockSpec(memory_space=pltpu.VMEM)
HBM = pl.BlockSpec(memory_space=pltpu.HBM)
SMEM = pl.BlockSpec(memory_space=pltpu.SMEM)
NT = (((1,), (1,)), ((), ()))
TN = (((0,), (0,)), ((), ()))


def norm_scale(values, gain):
    return values * lax.rsqrt(jnp.mean(values * values, axis=-1, keepdims=True) + EPS) * gain


def place():
    c = lax.axis_index("ctx")
    h = lax.axis_index("fsdp")
    return h, c // 32, (c // 8) % 4, (c // 2) % 4, c % 2


def device(h, xl, z, y, core):
    return {"ctx": xl * 32 + z * 8 + y * 2 + core, "fsdp": h}


def axis_neighbour(axis, step):
    h, xl, z, y, core = place()
    if axis == "x":
        x = (2 * h + xl + step) % 4
        return device(x // 2, x % 2, z, y, core)
    if axis == "y":
        return device(h, xl, z, (y + step) % 4, core)
    return device(h, xl, (z + step) % 4, y, core)


def sibling():
    h, xl, z, y, core = place()
    return device(h, xl, z, y, 1 - core)


def greet(devices):
    barrier = pltpu.get_barrier_semaphore()
    for d in devices:
        pl.semaphore_signal(barrier, inc=1, device_id=d, device_id_type=MESH)
    pl.semaphore_wait(barrier, len(devices))


class Links:
    def __init__(self, send_sems, recv_sems):
        self.send_sems, self.recv_sems, self.count = send_sems, recv_sems, 0

    def send(self, src, dst, target):
        i = self.count
        self.count += 1
        copy = pltpu.make_async_remote_copy(
            src_ref=src,
            dst_ref=dst,
            send_sem=self.send_sems.at[i],
            recv_sem=self.recv_sems.at[i],
            device_id=target,
            device_id_type=MESH,
        )
        copy.start()
        return copy


class GatherRing:
    def __init__(self, links, axis, me, items):
        self.links, self.items = links, items
        self.me, self.left, self.right = me, (me + 3) % 4, (me + 1) % 4
        self.to_left, self.to_right = axis_neighbour(axis, 3), axis_neighbour(axis, 1)

    def start(self):
        self.first = []
        for whole, half in self.items:
            mine = whole(self.me)
            self.first.append(
                (
                    self.links.send(mine, mine, self.to_right),
                    self.links.send(mine, mine, self.to_left),
                )
            )

    def relay(self):
        self.second = []
        for (whole, half), (a, b) in zip(self.items, self.first):
            a.wait_recv()
            piece = half(self.left, 0)
            c = self.links.send(piece, piece, self.to_right)
            b.wait_recv()
            piece = half(self.right, 1)
            d = self.links.send(piece, piece, self.to_left)
            self.second.append((c, d))

    def finish(self):
        for c, d in self.second:
            c.wait_recv()
            d.wait_recv()

    def drain(self):
        for pair in self.first + self.second:
            for copy in pair:
                copy.wait_send()


def ring_of(links, axis, me, *items):
    ring = GatherRing(links, axis, me, items)
    ring.start()
    return ring


class PairGather:
    def __init__(self, links, axis, me, axis2, me2, piece, swap):
        self.links, self.axis, self.me, self.axis2, self.me2 = links, axis, me, axis2, me2
        self.piece, self.swap = piece, swap
        self.firsts, self.seconds = [], []

    def half(self, ref, k):
        return ref.at[pl.ds(64 * k, 64)]

    def spread(self, p, i):
        here = lambda j: self.piece(p, i, j)
        ring = ring_of(
            self.links, self.axis2, self.me2, (here, lambda j, k: self.half(here(j), k))
        )
        self.swap(here(self.me2))
        self.seconds.append((ring, here))

    def begin(self, p):
        here = lambda i: self.piece(p, i, self.me2)
        self.firsts.append(
            ring_of(self.links, self.axis, self.me, (here, lambda i, k: self.half(here(i), k)))
        )
        self.spread(p, self.me)

    def middle(self, p):
        ring = self.firsts[0 if len(self.seconds) == 2 else 1]
        ring.relay()
        self.spread(p, (self.me + 3) % 4)
        self.spread(p, (self.me + 1) % 4)
        ring.finish()
        self.spread(p, (self.me + 2) % 4)

    def relay(self, k):
        ring, here = self.seconds[k]
        ring.relay()
        self.swap(here((self.me2 + 3) % 4))
        self.swap(here((self.me2 + 1) % 4))

    def finish(self, k):
        ring, here = self.seconds[k]
        ring.finish()
        self.swap(here((self.me2 + 2) % 4))

    def drain(self):
        for ring in self.firsts + [ring for ring, _ in self.seconds]:
            ring.drain()


def front_kernel(
    wq, wk, wv, wo, wg, wu, wd, inputs, gain_in, gain_query, gain_key, cosine, sine,
    oq, okv, oo, og, ou, od, k_all, v_all, act_out, query_lin_out, key_lin_out, query_out,
    send_sems, recv_sems, local_sems,
):
    h, xl, z, y, core = place()
    o = 1 - h
    cross = device(1 - h, 1 - xl, z, y, core)
    other = device(h, 1 - xl, z, y, core)
    locals_ = []
    for i, (src, dst) in enumerate(
        (
            (wq, oq.at[h]),
            (wk, okv.at[h, :, pl.ds(0, 256)]),
            (wv, okv.at[h, :, pl.ds(256, 256)]),
            (wg, og.at[h]),
            (wu, ou.at[h]),
            (wd, od.at[h]),
            (wo, oo.at[h]),
        )
    ):
        copy = pltpu.make_async_copy(src, dst, local_sems.at[i])
        copy.start()
        locals_.append(copy)
    greet(
        [cross, other, sibling()]
        + [axis_neighbour(a, s) for a in ("y", "z") for s in (1, 3)]
    )
    links = Links(send_sems, recv_sems)

    def rows(i, n):
        return pl.ds(pl.multiple_of(i * n, 16), n)

    def cols(start, n):
        return pl.ds(pl.multiple_of(start, 128), n)

    def piece_g(ref, yy, zz):
        return ref.at[rows(yy, 80), cols(core * 1024 + zz * 256, 256)]

    def piece_q(ref, yy, zz):
        return ref.at[rows(yy, 80), cols(core * 512 + zz * 128, 128)]

    def piece_kv(ref, yy, zz):
        return ref.at[rows(yy, 80), cols(zz * 128, 128)]

    def piece_d(ref, yy, zz):
        return ref.at[rows((core * 4 + zz) * 4 + yy, 32)]

    def piece_o(ref, yy, zz):
        return ref.at[rows((core * 4 + yy) * 4 + zz, 16)]

    for copy in locals_[3:]:
        copy.wait()
    crosses = [
        links.send(piece(dst.at[h], y, z), piece(dst.at[h], y, z), cross)
        for dst, piece in ((og, piece_g), (od, piece_d), (ou, piece_g), (oo, piece_o))
    ]
    for copy in locals_[:3]:
        copy.wait()
    half_q = lambda ref: ref.at[:, cols(core * 512, 512)]
    half_kv = lambda ref: ref.at[:, cols(core * 256, 256)]
    directs = [
        links.send(half_kv(okv.at[h]), half_kv(okv.at[h]), cross),
        links.send(half_q(oq.at[h]), half_q(oq.at[h]), cross),
    ]
    g, u, q, d, w, kv = og.at[o], ou.at[o], oq.at[o], od.at[o], oo.at[o], okv.at[o]
    rings = []
    swaps = []

    def swap(piece):
        swaps.append(links.send(piece, piece, sibling()))

    for copy in crosses[:2]:
        copy.wait_recv()
    a1 = ring_of(
        links, "y", y,
        (
            lambda i: piece_g(g, i, z),
            lambda i, k: g.at[rows(i, 80), cols(core * 1024 + z * 256 + k * 128, 128)],
        ),
        (
            lambda i: piece_d(d, i, z),
            lambda i, k: d.at[rows(((core * 4 + z) * 4 + i) * 2 + k, 16)],
        ),
    )
    for copy in crosses[2:]:
        copy.wait_recv()
    b1 = ring_of(
        links, "z", z,
        (
            lambda i: piece_g(u, y, i),
            lambda i, k: u.at[rows(y, 80), cols(core * 1024 + i * 256 + k * 128, 128)],
        ),
        (
            lambda i: piece_o(w, y, i),
            lambda i, k: w.at[
                rows((core * 4 + y) * 4 + i, 16), pl.ds(384 * k, 256 if k else 384)
            ],
        ),
    )
    for ring in (a1, b1):
        ring.relay()
    for ring in (a1, b1):
        ring.finish()
    a2 = ring_of(
        links, "z", z,
        (
            lambda i: g.at[:, cols(core * 1024 + i * 256, 256)],
            lambda i, k: g.at[pl.ds(160 * k, 160), cols(core * 1024 + i * 256, 256)],
        ),
        (
            lambda i: d.at[rows(core * 4 + i, 128)],
            lambda i, k: d.at[rows((core * 4 + i) * 2 + k, 64)],
        ),
    )
    b2 = ring_of(
        links, "y", y,
        (
            lambda i: u.at[rows(i, 80), cols(core * 1024, 1024)],
            lambda i, k: u.at[rows(i, 80), cols(core * 1024 + k * 512, 512)],
        ),
        (
            lambda i: w.at[rows(core * 4 + i, 64)],
            lambda i, k: w.at[rows((core * 4 + i) * 2 + k, 32)],
        ),
    )
    directs[0].wait_recv()
    swap(half_kv(kv))
    a2.relay()
    b2.relay()
    directs[1].wait_recv()
    swap(half_q(q))
    swaps[0].wait_recv()

    states = inputs[...].astype(F32)
    act = norm_scale(states, gain_in[...]).astype(BF16)
    act_out[...] = act
    kv_lin = jnp.dot(act, okv[...].reshape(640, 512), preferred_element_type=F32)
    key_lin_out[...] = kv_lin[:, :256]
    cos, sin = cosine[...], sine[...]

    def turned(lin, gain):
        n = norm_scale(lin, gain)
        a, b = n[:, :128], n[:, 128:]
        return jnp.concatenate([a * cos - b * sin, b * cos + a * sin], axis=1).astype(BF16)

    k_all[xl, z, y, core] = turned(kv_lin[:, :256], gain_key[...])
    v_all[xl, z, y, core] = kv_lin[:, 256:].astype(BF16)
    own = lambda ref: ref.at[xl, z, y, core]
    first = [links.send(own(ref), own(ref), other) for ref in (k_all, v_all)]
    keys = PairGather(links, "y", y, "z", z, lambda p, i, j: k_all.at[p, j, i, core], swap)
    values = PairGather(links, "z", z, "y", y, lambda p, i, j: v_all.at[p, i, j, core], swap)
    keys.begin(xl)
    values.begin(xl)
    swaps[1].wait_recv()
    for head in range(4):
        lin = jnp.dot(
            act,
            oq[:, :, head * 256 : (head + 1) * 256].reshape(640, 256),
            preferred_element_type=F32,
        )
        query_lin_out[:, head * 256 : (head + 1) * 256] = lin
        row = turned(lin, gain_query[...])
        query_out[head * 64 : (head + 1) * 64] = row[:64]
        query_out[256 + head * 64 : 256 + (head + 1) * 64] = row[64:]

    for copy, gather in zip(first, (keys, values)):
        copy.wait_recv()
        gather.begin(1 - xl)
    for gather in (keys, values):
        gather.middle(xl)
    for gather in (keys, values):
        gather.middle(1 - xl)
    a2.finish()
    b2.finish()
    swap(g.at[:, cols(core * 1024, 1024)])
    swap(u.at[:, cols(core * 1024, 1024)])
    swap(d.at[rows(core, 512)])
    swap(w.at[rows(core, 256)])
    for k in range(8):
        for gather in (keys, values):
            gather.relay(k)
    for k in range(8):
        for gather in (keys, values):
            gather.finish(k)
    for ring in (a1, b1, a2, b2, keys, values):
        ring.drain()
    for copy in crosses + directs + first:
        copy.wait_send()
    for copy in swaps[:2]:
        copy.wait_send()
    for copy in swaps[2:]:
        copy.wait()


def front(weights, inputs, gain_in, gain_query, gain_key, cosine, sine):
    wq, wk, wv, wo, wg, wu, wd = weights
    full = lambda rows, width: jax.ShapeDtypeStruct((2, rows, width), BF16)
    kv = jax.ShapeDtypeStruct((2, 4, 4, 2, 128, 256), BF16)
    count = 6 + 32 + 2 + 4 + 2 + 2 * (2 + 8) * 4 + 2 * 8 * 4
    outs = pl.pallas_call(
        front_kernel,
        name="front",
        out_shape=(
            full(320, 1024), full(320, 512), full(512, 640), full(320, 2048), full(320, 2048),
            full(1024, 640), kv, kv,
            jax.ShapeDtypeStruct((128, 640), BF16),
            jax.ShapeDtypeStruct((128, 1024), F32),
            jax.ShapeDtypeStruct((128, 256), F32),
            jax.ShapeDtypeStruct((512, 256), BF16),
        ),
        in_specs=[HBM] * 7 + [VMEM] * 6,
        out_specs=(VMEM,) * 12,
        scratch_shapes=[
            pltpu.SemaphoreType.DMA((count,)),
            pltpu.SemaphoreType.DMA((count,)),
            pltpu.SemaphoreType.DMA((7,)),
        ],
        compiler_params=pltpu.CompilerParams(
            collective_id=1, has_side_effects=True, vmem_limit_bytes=40 << 20
        ),
    )(*weights, inputs, gain_in[None], gain_query[None], gain_key[None], cosine, sine)
    flat = [o.reshape(2 * o.shape[1], o.shape[2]) for o in outs[:6]]
    return flat + [o.reshape(64, 128, 256) for o in outs[6:8]] + list(outs[8:])


def add_into(dst, src, lead):
    if not lead:
        dst[...] = (dst[...].astype(F32) + src[...].astype(F32)).astype(dst.dtype)
        return

    @pl.loop(0, lead[0])
    def _(i):
        add_into(dst.at[i], src.at[i], lead[1:])


def sum_into(dst, terms, lead):
    if not lead:
        total = terms[0][...].astype(F32)
        for t in terms[1:]:
            total = total + t[...].astype(F32)
        dst[...] = total.astype(dst.dtype)
        return

    @pl.loop(0, lead[0])
    def _(i):
        sum_into(dst.at[i], [t.at[i] for t in terms], lead[1:])


class SumRing:
    def __init__(self, links, axis, me, block, half, pass0, pass1, from_left, from_right, part, lead, half_lead):
        self.links = links
        self.me, self.left, self.right, self.far = me, (me + 3) % 4, (me + 1) % 4, (me + 2) % 4
        self.to_left, self.to_right = axis_neighbour(axis, 3), axis_neighbour(axis, 1)
        self.block, self.half = block, half
        self.pass0, self.pass1 = pass0, pass1
        self.from_left, self.from_right = from_left, from_right
        self.part, self.lead, self.half_lead = part, lead, half_lead

    def start(self, ready):
        send = self.links.send
        ready(self.far)
        self.a = send(self.half(self.far, 0), self.pass0, self.to_right)
        self.b = send(self.half(self.far, 1), self.pass1, self.to_left)
        ready(self.right)
        self.c = send(self.half(self.right, 1), self.part(self.from_left, 1), self.to_right)
        ready(self.left)
        self.d = send(self.half(self.left, 0), self.part(self.from_right, 0), self.to_left)
        ready(self.me)

    def relay(self):
        send = self.links.send
        self.a.wait_recv()
        add_into(self.half(self.right, 0), self.pass0, self.half_lead)
        self.e = send(self.half(self.right, 0), self.part(self.from_left, 0), self.to_right)
        self.b.wait_recv()
        add_into(self.half(self.left, 1), self.pass1, self.half_lead)
        self.f = send(self.half(self.left, 1), self.part(self.from_right, 1), self.to_left)

    def finish(self, out):
        for copy in (self.c, self.d, self.e, self.f):
            copy.wait_recv()
        sum_into(out, [self.block(self.me), self.from_left, self.from_right], self.lead)

    def drain(self):
        for copy in (self.a, self.b, self.c, self.d, self.e, self.f):
            copy.wait_send()


class Direct:
    def __init__(self, links, axis, me, block, got):
        self.links, self.axis, self.me, self.block, self.got = links, axis, me, block, got

    def start(self):
        self.copies = [
            self.links.send(
                self.block((self.me + step) % 4), self.got.at[step - 1], axis_neighbour(self.axis, step)
            )
            for step in (1, 2, 3)
        ]

    def finish(self, out):
        for copy in self.copies:
            copy.wait_recv()
        sum_into(out, [self.block(self.me)] + [self.got.at[i] for i in range(3)], ())

    def drain(self):
        for copy in self.copies:
            copy.wait_send()


def nothing(i):
    pass


def first_half(ref, k):
    return ref.at[pl.ds(2 * k, 2)]


class KeySum:
    SCRATCH = 12

    def __init__(self, links, source, out, scratch, axes):
        h, xl, z, y, core = place()
        self.links, self.source, self.out, self.axes = links, source, out, axes
        self.xl, self.core, self.me = xl, core, {"y": y, "z": z}
        self.got, self.p0, self.p1, self.fl, self.fr, self.second, self.q0, self.q1, self.gl, self.gr, self.third, self.last = scratch
        self.other = device(h, 1 - xl, z, y, core)

    @staticmethod
    def scratch():
        buf = lambda *lead: pltpu.VMEM(lead + (128, 256), BF16)
        return [buf(2, 4, 4), buf(4), buf(4), buf(2, 4), buf(2, 4), buf(2, 4), buf(), buf(), buf(2), buf(2), buf(2), buf()]

    def at(self, ref, i, *more):
        return ref.at[(slice(None), i, slice(None)) + more] if self.axes[0] == "z" else ref.at[(slice(None), slice(None), i) + more]

    def swap(self):
        me = self.me[self.axes[0]]
        self.swaps = [
            self.links.send(self.at(self.source, i, 1 - self.core), self.at(self.got, i), sibling())
            for i in ((me + 2) % 4, (me + 1) % 4, (me + 3) % 4, me)
        ]
        self.pending = list(self.swaps)

    def ready(self, i):
        self.pending.pop(0).wait_recv()
        mine, got = self.at(self.source, i, self.core), self.at(self.got, i)
        add_into(got, mine, (2, 4))

    def start(self):
        first, second = self.axes
        half = lambda i, k: self.got.at[(k, i) if first == "z" else (k, slice(None), i)]
        self.ring = SumRing(
            self.links, first, self.me[first], lambda i: self.at(self.got, i), half,
            self.p0, self.p1, self.fl, self.fr, lambda ref, k: ref.at[k], (2, 4), (4,),
        )
        self.ring2 = SumRing(
            self.links, second, self.me[second], lambda i: self.second.at[:, i],
            lambda i, k: self.second.at[k, i],
            self.q0, self.q1, self.gl, self.gr, lambda ref, k: ref.at[k], (2,), (),
        )
        self.ring.start(self.ready)

    def relay(self):
        self.ring.relay()

    def next(self):
        self.ring.finish(self.second)
        self.ring2.start(nothing)

    def relay2(self):
        self.ring2.relay()

    def next2(self):
        self.ring2.finish(self.third)
        self.copy = self.links.send(self.third.at[1 - self.xl], self.last, self.other)

    def finish(self):
        self.copy.wait_recv()
        sum_into(self.out, [self.third.at[self.xl], self.last], ())

    def drain(self):
        self.ring.drain()
        self.ring2.drain()
        for copy in self.swaps + [self.copy]:
            copy.wait_send()


class WeightSum:
    SCRATCH = 14

    def __init__(self, links, source, out, scratch, axes, local_sem):
        h, xl, z, y, core = place()
        self.links, self.source, self.out, self.axes = links, source, out, axes
        self.core, self.me = core, {"x": 2 * h + xl, "y": y, "z": z}
        (
            self.own, self.got, self.total, self.p0, self.p1, self.fl, self.fr,
            self.total2, self.q0, self.q1, self.gl, self.gr, self.total3, self.last,
        ) = scratch
        self.local = pltpu.make_async_copy(source.at[:, :, :, core], self.own, local_sem)
        self.local.start()

    @staticmethod
    def scratch(rows):
        buf = lambda *lead: pltpu.VMEM(lead + (rows, 128), BF16)
        return (
            [buf(2, 4, 4, 2)] * 2
            + [buf(4, 4, 4), buf(2, 4), buf(2, 4), buf(4, 4), buf(4, 4)]
            + [buf(4, 4), buf(2), buf(2), buf(4), buf(4), buf(4), buf(3)]
        )

    def at(self, ref, i, core=None):
        every = slice(None)
        mid = () if core is None else (core,)
        spot = {
            "x": (i % 2, every, every) + mid + (i // 2,),
            "y": (every, every, i) + mid,
            "z": (every, i, every) + mid,
        }[self.axes[0]]
        return ref.at[spot]

    def swap(self):
        me = self.me[self.axes[0]]
        self.swaps = [
            self.links.send(self.at(self.source, i, 1 - self.core), self.at(self.got, i), sibling())
            for i in ((me + 2) % 4, (me + 1) % 4, (me + 3) % 4, me)
        ]
        self.pending = list(self.swaps)

    def ready(self, i):
        self.pending.pop(0).wait_recv()

        @pl.loop(0, 4)
        def _(j):
            @pl.loop(0, 4)
            def _(k):
                spot = dict(zip(self.axes, (i, j, k)))
                x, y, z = spot["x"], spot["y"], spot["z"]
                where = (x % 2, z, y, x // 2)
                sum_into(self.total.at[i, j, k], [self.own.at[where], self.got.at[where]], ())

    def start(self):
        first, second, third = self.axes
        self.local.wait()
        self.ring = SumRing(
            self.links, first, self.me[first], lambda i: self.total.at[i],
            lambda i, k: first_half(self.total.at[i], k),
            self.p0, self.p1, self.fl, self.fr, first_half, (4, 4), (2, 4),
        )
        self.ring2 = SumRing(
            self.links, second, self.me[second], lambda i: self.total2.at[i],
            lambda i, k: first_half(self.total2.at[i], k),
            self.q0, self.q1, self.gl, self.gr, first_half, (4,), (2,),
        )
        self.direct = Direct(
            self.links, third, self.me[third], lambda i: self.total3.at[i], self.last
        )
        self.ring.start(self.ready)

    def relay(self):
        self.ring.relay()

    def next(self):
        self.ring.finish(self.total2)
        self.ring2.start(nothing)

    def relay2(self):
        self.ring2.relay()

    def next2(self):
        self.ring2.finish(self.total3)
        self.direct.start()

    def finish(self):
        self.direct.finish(self.out)

    def drain(self):
        self.ring.drain()
        self.ring2.drain()
        self.direct.drain()
        for copy in self.swaps:
            copy.wait_send()


def sum_kernel(orders, n_kv, *refs):
    n = n_kv + len(orders)
    sources, outs, rest = refs[:n], refs[n : 2 * n], list(refs[2 * n :])
    send_sems, recv_sems, local_sems = rest[-3:]
    h, xl, z, y, core = place()
    greet(
        [sibling()] + [axis_neighbour(a, s) for a in ("x", "y", "z") for s in (1, 2, 3)]
    )
    links = Links(send_sems, recv_sems)
    sums = []
    for t in range(n):
        if t < n_kv:
            scratch, rest = rest[: KeySum.SCRATCH], rest[KeySum.SCRATCH :]
            sums.append(KeySum(links, sources[t], outs[t], scratch, ("zy", "yz")[t]))
        else:
            scratch, rest = rest[: WeightSum.SCRATCH], rest[WeightSum.SCRATCH :]
            sums.append(
                WeightSum(
                    links, sources[t], outs[t], scratch, orders[t - n_kv], local_sems.at[t]
                )
            )
    for stage in ("swap", "start", "relay", "next", "relay2", "next2", "finish", "drain"):
        for s in sums:
            getattr(s, stage)()


def sum_up(name, collective_id, grads, orders, kv=()):
    scratch, outs, count = [], [], 0
    for _ in kv:
        scratch += KeySum.scratch()
        outs.append(jax.ShapeDtypeStruct((128, 256), F32))
        count += 4 + 12 + 1
    for g in grads:
        scratch += WeightSum.scratch(g.shape[1])
        outs.append(jax.ShapeDtypeStruct(g.shape[1:], F32))
        count += 4 + 12 + 3
    n = len(outs)
    return pl.pallas_call(
        functools.partial(sum_kernel, orders, len(kv)),
        name=name,
        out_shape=tuple(outs),
        in_specs=[VMEM] * len(kv) + [HBM] * len(grads),
        out_specs=(VMEM,) * n,
        scratch_shapes=scratch
        + [
            pltpu.SemaphoreType.DMA((count,)),
            pltpu.SemaphoreType.DMA((count,)),
            pltpu.SemaphoreType.DMA((n,)),
        ],
        compiler_params=pltpu.CompilerParams(
            collective_id=collective_id, has_side_effects=True, vmem_limit_bytes=40 << 20
        ),
    )(
        *[g.reshape((2, 4, 4, 2) + g.shape[1:]) for g in kv],
        *[g.reshape((2, 4, 4, 2, 2) + g.shape[1:]) for g in grads],
    )


def tile(ref, inverse, step):
    parts = []
    for j in range(8):
        block = step * 8 + j
        late = block >= 64
        owner = inverse[jnp.where(late, 127 - block, block)]
        half = pl.multiple_of(jnp.where(late, 64, 0), 64)
        parts.append(ref[owner, pl.ds(half, 64), :])
    return jnp.concatenate(parts, axis=0)


def attention_kernel(inverse, pair, query, keys, values, out, sums, acc, weight):
    own = pair[0]

    def rows_of(part):
        return pl.ds(part * 256, 256)

    acc[...] = jnp.zeros_like(acc)
    weight[...] = jnp.zeros_like(weight)

    def step_for(part, block, step, masked):
        k = tile(keys, inverse, step)
        v = tile(values, inverse, step)
        q = query[rows_of(part), :]
        raw = lax.dot_general(q, k, NT, preferred_element_type=F32)
        p = jnp.exp2(raw * EXP2_SCALE)
        if masked:
            token = lax.broadcasted_iota(jnp.int32, (256, 512), 0) % 64 + block * 64
            position = lax.broadcasted_iota(jnp.int32, (256, 512), 1) + step * 512
            p = jnp.where(position <= token, p, 0.0)
        w = p[:, :128] + p[:, 128:256] + p[:, 256:384] + p[:, 384:]
        weight[rows_of(part), :] += w
        acc[rows_of(part), :] += jnp.dot(p.astype(BF16), v, preferred_element_type=F32)

    for part in range(2):
        block = own if part == 0 else 127 - own
        full = block // 8

        @pl.loop(0, full)
        def _(step):
            step_for(part, block, step, False)

        step_for(part, block, full, True)
    total = jnp.sum(weight[...], axis=1, keepdims=True)
    out[...] = acc[...] / total
    sums[...] = total


def attention(inverse, pair, query, keys, values):
    return pl.pallas_call(
        attention_kernel,
        name="attention_forward",
        out_shape=(
            jax.ShapeDtypeStruct((512, 256), F32),
            jax.ShapeDtypeStruct((512, 1), F32),
        ),
        in_specs=[SMEM, SMEM, VMEM, VMEM, VMEM],
        out_specs=(VMEM, VMEM),
        scratch_shapes=[pltpu.VMEM((512, 256), F32), pltpu.VMEM((512, 128), F32)],
        compiler_params=pltpu.CompilerParams(vmem_limit_bytes=10 << 20),
    )(inverse, pair, query, keys, values)


def attention_back_kernel(
    inverse, pair, query, d_out, log_sum, delta, keys, values, d_query, d_keys, d_values
):
    own = pair[0]
    d_query[...] = jnp.zeros_like(d_query)

    def terms(part, step, k, v, masked):
        rows = pl.ds(part * 256, 256)
        block = own if part == 0 else 127 - own
        q = query[rows, :]
        g = d_out[rows, :]
        raw = lax.dot_general(k, q, NT, preferred_element_type=F32)
        p = jnp.exp2(raw * EXP2_SCALE - log_sum[:, rows])
        if masked:
            position = lax.broadcasted_iota(jnp.int32, (512, 256), 0) + step * 512
            token = lax.broadcasted_iota(jnp.int32, (512, 256), 1) % 64 + block * 64
            p = jnp.where(position <= token, p, 0.0)
        d_p = lax.dot_general(v, g, NT, preferred_element_type=F32)
        d_s = (p * (d_p - delta[:, rows])).astype(BF16)
        d_query[rows, :] += lax.dot_general(d_s, k, TN, preferred_element_type=F32)
        d_k = jnp.dot(d_s, q, preferred_element_type=F32)
        d_v = jnp.dot(p.astype(BF16), g, preferred_element_type=F32)
        return d_k, d_v

    def store(step, d_k, d_v):
        for j in range(8):
            block = step * 8 + j
            late = block >= 64
            owner = inverse[jnp.where(late, 127 - block, block)]
            half = pl.multiple_of(jnp.where(late, 64, 0), 64)
            d_keys[owner, pl.ds(half, 64), :] = (d_k[j * 64 : (j + 1) * 64] * SCALE).astype(BF16)
            d_values[owner, pl.ds(half, 64), :] = d_v[j * 64 : (j + 1) * 64].astype(BF16)

    early_full = own // 8
    late_full = (127 - own) // 8

    @pl.loop(0, early_full)
    def _(step):
        k = tile(keys, inverse, step)
        v = tile(values, inverse, step)
        d_k, d_v = terms(1, step, k, v, False)
        d_k2, d_v2 = terms(0, step, k, v, False)
        store(step, d_k + d_k2, d_v + d_v2)

    k = tile(keys, inverse, early_full)
    v = tile(values, inverse, early_full)
    d_k, d_v = terms(1, early_full, k, v, False)
    d_k2, d_v2 = terms(0, early_full, k, v, True)
    store(early_full, d_k + d_k2, d_v + d_v2)

    @pl.loop(early_full + 1, late_full)
    def _(step):
        d_k, d_v = terms(1, step, tile(keys, inverse, step), tile(values, inverse, step), False)
        store(step, d_k, d_v)

    d_k, d_v = terms(
        1, late_full, tile(keys, inverse, late_full), tile(values, inverse, late_full), True
    )
    store(late_full, d_k, d_v)
    zero = jnp.zeros((512, 256), F32)

    @pl.loop(late_full + 1, 16)
    def _(step):
        store(step, zero, zero)

    d_query[...] = d_query[...] * SCALE


def attention_back(inverse, pair, query, d_out, log_sum, delta, keys, values):
    return pl.pallas_call(
        attention_back_kernel,
        name="attention_backward",
        out_shape=(
            jax.ShapeDtypeStruct((512, 256), F32),
            jax.ShapeDtypeStruct(keys.shape, BF16),
            jax.ShapeDtypeStruct(keys.shape, BF16),
        ),
        in_specs=[SMEM, SMEM] + [VMEM] * 6,
        out_specs=(VMEM,) * 3,
        compiler_params=pltpu.CompilerParams(vmem_limit_bytes=10 << 20),
    )(inverse, pair, query, d_out, log_sum, delta, keys, values)


def rotate(values, angles):
    half = values.shape[-1] // 2
    first = values[..., :half]
    second = values[..., half:]
    cosine = jnp.cos(angles)
    sine = jnp.sin(angles)
    return jnp.concatenate(
        [first * cosine - second * sine, second * cosine + first * sine], axis=-1
    )


def head_rows(values):
    return values.reshape(2, 64, 4, 256).transpose(0, 2, 1, 3).reshape(512, 256)


def token_rows(values):
    return values.reshape(2, 4, 64, 256).transpose(0, 2, 1, 3).reshape(128, 1024)


def local(
    inputs,
    pair_order,
    w_query,
    w_key,
    w_value,
    w_output,
    w_gate,
    w_up,
    w_down,
    gain_in,
    gain_query,
    gain_key,
    gain_post_attn,
    gain_pre_ff,
    gain_post_ff,
    cotangent,
):
    f32, bf16 = F32, BF16
    rows = 128
    me_index = lax.axis_index("ctx")
    own_pair = lax.dynamic_slice_in_dim(pair_order, me_index, 1)
    within = jnp.arange(rows, dtype=jnp.int32)
    block_id = jnp.where(within < 64, own_pair, 127 - own_pair)
    positions = block_id * 64 + within % 64
    freq = ROPE_BASE ** (-jnp.arange(128, dtype=f32) / 128)
    angles = positions.astype(f32)[:, None] * freq
    matches = pair_order[None, :] == jnp.arange(64, dtype=jnp.int32)[:, None]
    inverse = jnp.sum(jnp.where(matches, jnp.arange(64, dtype=jnp.int32)[None, :], 0), axis=1)

    def prepare(query_lin, key_lin, g_query, g_key):
        query = rotate(
            norm_scale(query_lin.reshape(rows, 4, 256), g_query), angles[:, None, :]
        )
        key = rotate(norm_scale(key_lin, g_key), angles)
        return (query, key)

    states = inputs[0].astype(f32)
    (
        wq_all, wkv_all, wo_all, wg_all, wu_all, wd_all, k_all, v_all,
        act_one, query_lin, key_lin, query_b,
    ) = front(
        (w_query, w_key, w_value, w_output, w_gate, w_up, w_down),
        inputs[0], gain_in, gain_query, gain_key, jnp.cos(angles), jnp.sin(angles),
    )
    attended, weight_sum = attention(inverse, own_pair, query_b, k_all, v_all)
    attended_flat = token_rows(attended.astype(bf16))
    att_lin = jnp.dot(attended_flat, wo_all, preferred_element_type=f32)
    resid = states + norm_scale(att_lin, gain_post_attn)
    act_two = norm_scale(resid, gain_pre_ff).astype(bf16)
    gate = jnp.dot(act_two, wg_all, preferred_element_type=f32)
    upper = jnp.dot(act_two, wu_all, preferred_element_type=f32)
    hidden_b = (jax.nn.gelu(gate, approximate=True) * upper).astype(bf16)
    down = jnp.dot(hidden_b, wd_all, preferred_element_type=f32)
    layer_out = resid + norm_scale(down, gain_post_ff)
    grad_y = cotangent[0].astype(f32)
    unused_out, post_ff_back = jax.vjp(norm_scale, down, gain_post_ff)
    d_down, d_gain_post_ff = post_ff_back(grad_y)
    d_down_b = d_down.astype(bf16)
    grad_down = jnp.einsum("rf,rd->fd", hidden_b, d_down_b, preferred_element_type=f32)
    d_hidden = jnp.einsum("rd,fd->rf", d_down_b, wd_all, preferred_element_type=f32)
    unused_act, act_back = jax.vjp(
        lambda gate_in, up_in: jax.nn.gelu(gate_in, approximate=True) * up_in, gate, upper
    )
    d_gate, d_upper = act_back(d_hidden)
    d_gate_b = d_gate.astype(bf16)
    d_upper_b = d_upper.astype(bf16)
    grad_gate = jnp.einsum("rd,rf->df", act_two, d_gate_b, preferred_element_type=f32)
    grad_up = jnp.einsum("rd,rf->df", act_two, d_upper_b, preferred_element_type=f32)
    d_act_two = jnp.einsum("rf,df->rd", d_gate_b, wg_all, preferred_element_type=f32) + jnp.einsum(
        "rf,df->rd", d_upper_b, wu_all, preferred_element_type=f32
    )
    unused_two, pre_ff_back = jax.vjp(norm_scale, resid, gain_pre_ff)
    d_resid_part, d_gain_pre_ff = pre_ff_back(d_act_two)
    grad_resid = grad_y + d_resid_part
    unused_three, post_attn_back = jax.vjp(norm_scale, att_lin, gain_post_attn)
    d_att, d_gain_post_attn = post_attn_back(grad_resid)
    d_att_b = d_att.astype(bf16)
    grad_output = jnp.einsum("re,rd->ed", attended_flat, d_att_b, preferred_element_type=f32)
    d_attended_b = head_rows(
        jnp.einsum("rd,ed->re", d_att_b, wo_all, preferred_element_type=f32).astype(bf16)
    )
    row_delta = jnp.sum(d_attended_b.astype(f32) * attended, axis=1)
    d_query_rows, d_keys, d_values = attention_back(
        inverse,
        own_pair,
        query_b,
        d_attended_b,
        jnp.log2(weight_sum).reshape(1, 512),
        row_delta[None, :],
        k_all,
        v_all,
    )
    split = lambda g: g.astype(bf16).reshape(128, -1, 128)
    d_key_own, d_value_own, s_down, s_gate, s_up, s_output = sum_up(
        "sum_first",
        3,
        [split(grad_down), split(grad_gate), split(grad_up), split(grad_output)],
        ("xyz", "xzy", "yzx", "zxy"),
        (d_keys, d_values),
    )
    d_value_b = d_value_own.astype(bf16)
    d_query = token_rows(d_query_rows).reshape(rows, 4, 256)
    unused_four, prep_back = jax.vjp(prepare, query_lin, key_lin, gain_query, gain_key)
    d_query_lin, d_key_lin, d_gain_query, d_gain_key = prep_back((d_query, d_key_own))
    d_query_lin_b = d_query_lin.astype(bf16).reshape(rows, 1024)
    d_kv_lin_b = jnp.concatenate([d_key_lin.astype(bf16), d_value_b], axis=1)
    grad_query = jnp.einsum("rd,re->de", act_one, d_query_lin_b, preferred_element_type=f32)
    grad_kv = jnp.einsum("rd,re->de", act_one, d_kv_lin_b, preferred_element_type=f32)
    d_act_one = jnp.einsum("re,de->rd", d_query_lin_b, wq_all, preferred_element_type=f32)
    d_act_one = d_act_one + jnp.einsum("re,de->rd", d_kv_lin_b, wkv_all, preferred_element_type=f32)
    unused_five, pre_attn_back = jax.vjp(norm_scale, states, gain_in)
    d_states, d_gain_in = pre_attn_back(d_act_one)
    input_grad = grad_resid + d_states

    gains = jnp.concatenate(
        [
            g.reshape(128, -1)
            for g in (
                d_gain_in,
                d_gain_post_attn,
                d_gain_pre_ff,
                d_gain_post_ff,
                d_gain_query,
                d_gain_key,
            )
        ],
        axis=1,
    )
    gains = jnp.pad(gains, ((0, 0), (0, 128 - gains.shape[1]))).astype(bf16)[:, None, :]
    tail = jnp.concatenate([split(grad_kv), gains, jnp.zeros((128, 11, 128), bf16)], axis=1)
    s_query, s_tail = sum_up("sum_last", 4, [split(grad_query), tail], ("xyz", "yzx"))
    s_down = s_down.reshape(16, 640)
    s_gate = s_gate.reshape(5, 2048)
    s_up = s_up.reshape(5, 2048)
    s_output = s_output.reshape(8, 640)
    s_query = s_query.reshape(5, 1024)
    s_kv = s_tail[:20].reshape(5, 512)
    s_gains = s_tail[20]
    return (
        layer_out.astype(bf16)[None],
        input_grad.astype(bf16)[None],
        s_query,
        s_kv[:, :256],
        s_kv[:, 256:],
        s_output,
        s_gate,
        s_up,
        s_down,
        s_gains[0:5],
        s_gains[20:22],
        s_gains[22:24],
        s_gains[5:10],
        s_gains[10:15],
        s_gains[15:20],
    )


def solution(mesh):
    placed = (
        P("fsdp", "ctx", None),
        P(),
        P("fsdp", None),
        P("fsdp", None),
        P("fsdp", None),
        P("fsdp", None),
        P("fsdp", None),
        P("fsdp", None),
        P("fsdp", None),
        P(),
        P(),
        P(),
        P(),
        P(),
        P(),
        P("fsdp", "ctx", None),
    )
    both = ("ctx", "fsdp")
    return jax.shard_map(
        local,
        mesh=mesh,
        in_specs=placed,
        out_specs=(P("fsdp", "ctx", None),) * 2 + (P(both, None),) * 7 + (P(both),) * 6,
        check_vma=False,
    )
```

time: 2120 us -> 274 us (0.13)
  waiting for transfers between devices: 1630 us -> 0 us
  matrix products: 220 us -> 20 us
  Pallas kernels: 0 us -> 170 us
  blocking collectives: 85.1 us -> 0 us
  other arithmetic: 54.6 us -> 10.1 us
  local copies, waits for them, and re-layouts: 105 us -> 70.2 us
    reduce_scatter x3 -> x0, waiting for transfers between devices: 1210 us -> none  [the longest x1 640 us: local(): lax.psum_scatter(grad_down, ('ctx', 'fsdp'), scatter_dimension=0, tiled=T...]
    all_gather x7 -> x0, waiting for transfers between devices: 267 us -> none  [the longest x1 105 us: local(): lax.all_gather(key_b, 'ctx', axis=0, tiled=True)]
    dot_general x126 -> x2, matrix products: 190 us -> 1.96 us  [the longest x1 1.61 us: local(): jnp.einsum('re,de->rd', d_kv_lin_b, wkv_all, preferred_element_type=f32)]
    pallas_call x0 -> x5, Pallas kernels: none -> 170 us  [the longest x2 77.8 us: sum_up(): pl.pallas_call(functools.partial(sum_kernel, orders, len(kv)), name=name,...]
    unnamed x12 -> x0, waiting for transfers between devices: 151 us -> none
    unnamed x1 -> x0, blocking collectives: 64.5 us -> none
    gather x9 -> x0, local copies, waits for them, and re-layouts: 32.8 us -> none  [the longest x2 9.95 us: to_device_order(): late = jnp.take(grouped[ndev:][::-1], pair_order, axis=0)]
  transfers between devices with their start and end apart: 11 -> 0, of which waited for: 9 -> 0; matrix products, arithmetic and copies ran while one was open for 7% -> 0% of each run, Pallas kernels for 0% -> 0%
where the time goes in v1:
time: 274 us; the launch traced here: 272 us
  Pallas kernels  170 us (62%)
  local copies, waits for them, and re-layouts  70.2 us (26%)
  matrix products  20 us (7%)
  other arithmetic  10.1 us (4%)
    pallas_call x2, Pallas kernels, sum_up(): pl.pallas_call(functools.partial(sum_kernel, orders, len(kv)), name=name,...  77.8 us
    pallas_call x1, Pallas kernels, front(): pl.pallas_call(front_kernel, name='front', out_shape=(full(320, 1024), fu...  69.2 us
    unnamed x141, local copies, waits for them, and re-layouts  37.2 us
    another operation x5, local copies, waits for them, and re-layouts, sum_up(): g.reshape((2, 4, 4, 2, 2) + g.shape[1:])  18.2 us
    pallas_call x1, Pallas kernels, attention_back(): pl.pallas_call(attention_back_kernel, name='attention_backward', out_shap...  13.8 us
    pallas_call x1, Pallas kernels, attention(): pl.pallas_call(attention_kernel, name='attention_forward', out_shape=(jax...  9.07 us

profile of v1, /device:TPU:0, one launch (start us, length us, event | category | flops | bytes accessed | tf_op | source)
XLA Modules:
  0.0 272.3 jit_solution(9250843636165784627)
XLA Ops:
  0.6 1.2 dynamic_slice.3.pair
  5.6 0.9 copy-done.13
  6.6 1.3 copy-done.19
  7.9 1.3 copy-done.20
  9.2 1.3 copy-done.21
  10.5 1.1 copy-done.26
  11.6 1.1 copy-done.27
  12.7 0.9 copy-done.33
  13.6 0.9 copy-done.34
  15.9 69.2 %front.1 = (bf16[2,320,1024]{2,1,0:T(8,128)(2,1)S(1)}, bf16[2,320,512]{2,1,0:T(8,128)(2,1)S(1)}, bf16[2,512,640]{2,1,0:T(8,128)(2,1)S(1)}, bf16[2,320,2048]{2,1,...) custom-call(bf16[320,1024]{1,0:T(8,128)(2,1)S(1)} %copy-done.26, ...), custom_call_target="tpu_custom_call" | custom-call | tf_op jit(solution)/shard_map/front/pallas_call | solution.py:374
  85.1 1.1 copy-done.7
  86.2 1.1 copy-done.17
  88.0 0.8 copy-done.25
  90.1 1.0 reshape.350
  91.1 1.3 multiply_reduce_fusion
  92.5 2.2 copy-done
  94.7 2.2 copy-done.2
  96.9 0.9 copy-done.23
  97.8 9.1 %attention_forward.1 = (f32[512,256]{1,0:T(8,128)S(1)}, f32[512,1]{1,0:T(8,128)S(1)}) custom-call(s32[64]{0:T(128)S(1)} %select_reduce_fusion.inverse, s32[1]{0:T(128)} %dynamic_slice.3.pair, bf16[512,256]{1,0:T(8,128)(2,1)S(1)} %copy-done.23, bf16[64,128,256]{2,1,0:T(8,128)(2,1)S(1)} %bitcast.104, bf16[64,128,256]{2,1,0:T(8,128)(2,1)S(1)} %bitcast.106), custom_call_target="tpu_custom_call" | custom-call | tf_op jit(solution)/shard_map/attention_forward/pallas_call | solution.py:766
  113.2 1.3 multiply_convert_fusion
  114.6 0.9 fusion.39
  115.5 1.1 multiply_reduce_fusion.2
  118.1 2.2 copy-done.1
  120.3 2.2 copy-done.3
  122.5 13.8 %attention_backward.1 = (f32[512,256]{1,0:T(8,128)S(1)}, bf16[64,128,256]{2,1,0:T(8,128)(2,1)S(1)}, bf16[64,128,256]{2,1,0:T(8,128)(2,1)S(1)}) custom-call(s32[64]{0:T(128)S(1)} %select_reduce_fusion.inverse, s32[1]{0:T(128)} %dynamic_slice.3.pair, bf16[512,256]{1,0:T(8,128)(2,1)S(1)} %copy-done.24, bf16[512,256]{1,0:T(8,128)(2,1)S(1)} %bitcast.117, ...), custom_call_target="tpu_custom_call" | custom-call | tf_op jit(solution)/shard_map/attention_backward/pallas_call | solution.py:849
  136.3 2.0 copy-done.10
  138.2 2.0 copy-done.12
  140.7 0.9 fusion.7
  141.6 1.1 copy.101
  142.7 1.3 fusion.40
  144.3 0.9 reshape.357
  147.3 2.0 reshape_reshape.22.refs_5_
  149.8 1.4 reshape_reshape.23.refs_0_
  151.3 2.4 convolution_convert_fusion
  153.7 3.9 %reshape_reshape.21.refs_4_ = bf16[2,4,4,2,2,80,128]{6,5,4,3,2,1,0:T(8,128)(2,1)S(1)} reshape(bf16[640,2048]{1,0:T(8,128)(2,1)} %convolution_convert_fusion) | data formatting | bytes 5242880 | tf_op jit(solution)/shard_map/reshape;reshape | solution.py:713
  157.6 3.5 %convolution_convert_fusion.1 = bf16[640,2048]{1,0:T(8,128)(2,1)} fusion(bf16[128,640]{1,0:T(8,128)(2,1)S(1)} %copy-done.44, bf16[128,2048]{1,0:T(8,128)(2,1)} %copy-done.52), kind=kOutput, calls=%fused_computation.1 | convolution fusion | flops 336855040 | bytes 3309568 | tf_op jit(solution)/shard_map/rd,rf->df/dot_general | solution.py:949
  161.1 5.3 %reshape_reshape.20.refs_3_ = bf16[2,4,4,2,2,80,128]{6,5,4,3,2,1,0:T(8,128)(2,1)} reshape(bf16[640,2048]{1,0:T(8,128)(2,1)} %convolution_convert_fusion.1) | data formatting | bytes 5242880 | tf_op jit(solution)/shard_map/reshape;reshape | solution.py:713
  166.5 3.3 %convolution_convert_fusion.2 = bf16[2048,640]{1,0:T(8,128)(2,1)} fusion(bf16[128,2048]{1,0:T(8,128)(2,1)S(1)} %copy-done.41, bf16[128,640]{1,0:T(8,128)(2,1)} %copy-done.54), kind=kOutput, calls=%fused_computation.2 | convolution fusion | flops 336855040 | bytes 3309568 | tf_op jit(solution)/shard_map/rf,rd->fd/dot_general | solution.py:941
  169.8 5.5 %reshape_reshape.19.refs_2_ = bf16[2,4,4,2,2,80,128]{6,5,4,3,2,1,0:T(8,128)(2,1)} reshape(bf16[2048,640]{1,0:T(8,128)(2,1)} %convolution_convert_fusion.2) | data formatting | bytes 5242880 | tf_op jit(solution)/shard_map/reshape;reshape | solution.py:713
  175.2 1.7 copy-done.4
  177.0 1.7 copy-done.5
  178.7 1.3 copy-done.6
  180.0 2.2 copy-done.11
  182.2 55.2 %sum_first.1 = (f32[128,256]{1,0:T(8,128)S(1)}, f32[128,256]{1,0:T(8,128)S(1)}, f32[80,128]{1,0:T(8,128)S(1)}, f32[80,128]{1,0:T(8,128)S(1)}, f32[80,128]{1,0:T(8,128)S(1)}, /*index=5*/f32[40,128]{1,0:T(8,128)S(1)}) custom-call(bf16[2,4,4,2,128,256]{5,4,3,2,1,0:T(8,128)(2,1)S(1)} %bitcast.114, bf16[2,4,4,2,128,256]{5,4,3,2,1,0:T(8,128)(2,1)} %bitcast.115, ...), custom_call_target="tpu_custom_call" | custom-call | tf_op jit(solution)/shard_map/sum_first/pallas_call | solution.py:696
  239.6 1.6 fusion.22
  244.1 1.4 concatenate.16
  245.6 1.6 maximum_maximum_fusion.refs_1_
  247.2 22.6 %sum_last.1 = (f32[40,128]{1,0:T(8,128)S(1)}, f32[32,128]{1,0:T(8,128)S(1)}) custom-call(bf16[2,4,4,2,2,40,128]{6,5,4,3,2,1,0:T(8,128)(2,1)S(1)} %copy-done.9, bf16[2,4,4,2,2,32,128]{6,5,4,3,2,1,0:T(8,128)(2,1)S(1)} %maximum_maximum_fusion.refs_1_), custom_call_target="tpu_custom_call" | custom-call | tf_op jit(solution)/shard_map/sum_last/pallas_call | solution.py:696
  (185 shorter events, 24.6 us)
Async XLA Ops:
  4.0 1.6 copy-start.62
  5.6 79.5 %copy-start.31 = (f32[128,128]{1,0:T(8,128)}, f32[128,128]{1,0:T(8,128)S(1)}, u32[]{:S(2)}) copy-start(f32[128,128]{1,0:T(8,128)S(1)} %get-tuple-element.98.cosine) | copy-start | bytes 196612
  6.6 1.3 copy-start.19
  89.6 2.9 %copy-start.68 = (f32[128]{0:T(128)}, f32[128]{0:T(128)S(1)}, u32[]{:S(2)}) copy-start(f32[128]{0:T(128)S(1)} %multiply_reduce_fusion.12) | copy-start | bytes 1540
  92.5 2.2 copy-start
  94.7 2.2 copy-start.2
  97.8 9.6 %copy-start.8 = (bf16[2,512,640]{2,1,0:T(8,128)(2,1)S(1)}, bf16[2,512,640]{2,1,0:T(8,128)(2,1)}, u32[]{:S(2)}) copy-start(bf16[2,512,640]{2,1,0:T(8,128)(2,1)} %copy-done.7) | copy-start | bytes 3932164
  106.9 1.5 copy-start.15
  106.9 1.3 copy-start.58
  107.9 1.8 copy-start.39
  108.2 8.4 %copy-start.65 = (f32[128]{0:T(128)}, f32[128]{0:T(128)S(1)}, u32[]{:S(2)}) copy-start(f32[128]{0:T(128)S(1)} %get-tuple-element.86) | copy-start | bytes 1540
  108.4 2.2 copy-start.42
  109.7 1.7 copy-start.47
  110.6 1.6 copy-start.53
  110.6 1.6 copy-start.61
  113.2 1.3 copy-start.54
  114.5 2.0 copy-start.50
  114.5 2.0 copy-start.52
  116.6 1.4 copy-start.24
  118.1 2.2 copy-start.1
  120.3 2.2 copy-start.3
  122.5 17.8 %copy-start.32 = (f32[128,128]{1,0:T(8,128)S(1)}, f32[128,128]{1,0:T(8,128)}, u32[]{:S(2)}) copy-start(f32[128,128]{1,0:T(8,128)} %copy-done.31) | copy-start | bytes 196612
  122.5 17.9 %copy-start.38 = (f32[256]{0:T(256)S(1)}, f32[256]{0:T(256)}, u32[]{:S(2)}) copy-start(f32[256]{0:T(256)} %param.26) | copy-start | bytes 3076
  136.3 2.0 copy-start.10
  138.2 2.0 copy-start.12
  140.2 2.5 copy-start.18
  140.4 6.4 %copy-start.49 = (bf16[16,8,4,256]{3,1,2,0:T(8,128)(2,1)S(1)}, bf16[16,8,4,256]{3,1,2,0:T(8,128)(2,1)}, u32[]{:S(2)}) copy-start(bf16[16,8,4,256]{3,1,2,0:T(8,128)(2,1)} %copy-done.48) | copy-start | bytes 786436
  144.0 5.3 %copy-start.29 = (bf16[128,640]{1,0:T(8,128)(2,1)S(1)}, bf16[128,640]{1,0:T(8,128)(2,1)}, u32[]{:S(2)}) copy-start(bf16[128,640]{1,0:T(8,128)(2,1)} %copy-done.28) | copy-start | bytes 491524
  149.3 2.0 copy-start.43
  149.3 2.0 copy-start.51
  153.7 3.9 %copy-start.44 = (bf16[128,640]{1,0:T(8,128)(2,1)S(1)}, bf16[128,640]{1,0:T(8,128)(2,1)}, u32[]{:S(2)}) copy-start(bf16[128,640]{1,0:T(8,128)(2,1)} %copy-done.42) | copy-start | bytes 491524
  161.1 5.3 %copy-start.41 = (bf16[128,2048]{1,0:T(8,128)(2,1)S(1)}, bf16[128,2048]{1,0:T(8,128)(2,1)}, u32[]{:S(2)}) copy-start(bf16[128,2048]{1,0:T(8,128)(2,1)} %copy-done.40) | copy-start | bytes 1572868
  175.2 1.7 copy-start.4
  177.0 1.7 copy-start.5
  180.0 2.2 copy-start.11
  182.2 55.3 %copy-start.63 = (f32[128]{0:T(128)S(1)}, f32[128]{0:T(128)}, u32[]{:S(2)}) copy-start(f32[128]{0:T(128)} %copy-done.62) | copy-start | bytes 1540
  182.2 55.6 %copy-start.36 = (f32[256]{0:T(256)S(1)}, f32[256]{0:T(256)}, u32[]{:S(2)}) copy-start(f32[256]{0:T(256)} %param.27) | copy-start | bytes 3076
  182.2 55.6 %copy-start.64 = (f32[128]{0:T(128)S(1)}, f32[128]{0:T(128)}, u32[]{:S(2)}) copy-start(f32[128]{0:T(128)} %fusion.33) | copy-start | bytes 1540
  182.2 55.8 %copy-start.69 = (f32[128]{0:T(128)S(1)}, f32[128]{0:T(128)}, u32[]{:S(2)}) copy-start(f32[128]{0:T(128)} %copy-done.68) | copy-start | bytes 1540
  182.2 57.3 %copy-start.60 = (f32[640]{0:T(1024)S(1)}, f32[640]{0:T(1024)}, u32[]{:S(2)}) copy-start(f32[640]{0:T(1024)} %param.25) | copy-start | bytes 7684
  237.4 3.8 %copy-start.66 = (f32[128]{0:T(128)S(1)}, f32[128]{0:T(128)}, u32[]{:S(2)}) copy-start(f32[128]{0:T(128)} %copy-done.65) | copy-start | bytes 1540
  237.4 3.8 %copy-start.46 = (f32[128,640]{1,0:T(8,128)S(1)}, f32[128,640]{1,0:T(8,128)}, u32[]{:S(2)}) copy-start(f32[128,640]{1,0:T(8,128)} %copy-done.45) | copy-start | bytes 983044
  237.4 4.8 %copy-start.55 = (bf16[128,5]{1,0:T(8,128)(2,1)S(1)}, bf16[128,5]{1,0:T(8,128)(2,1)}, u32[]{:S(2)}) copy-start(bf16[128,5]{1,0:T(8,128)(2,1)} %reshape.357) | copy-start | bytes 3844
  237.5 4.8 %copy-start.56 = (bf16[128,5]{1,0:T(8,128)(2,1)S(1)}, bf16[128,5]{1,0:T(8,128)(2,1)}, u32[]{:S(2)}) copy-start(bf16[128,5]{1,0:T(8,128)(2,1)} %reshape.358) | copy-start | bytes 3844
  237.5 4.8 %copy-start.57 = (bf16[128,2]{1,0:T(8,128)(2,1)S(1)}, bf16[128,2]{1,0:T(8,128)(2,1)}, u32[]{:S(2)}) copy-start(bf16[128,2]{1,0:T(8,128)(2,1)} %reshape.359) | copy-start | bytes 1540
  237.5 6.3 %copy-start.30 = (bf16[128,640]{1,0:T(8,128)(2,1)S(1)}, bf16[128,640]{1,0:T(8,128)(2,1)}, u32[]{:S(2)}) copy-start(bf16[128,640]{1,0:T(8,128)(2,1)} %copy-done.28) | copy-start | bytes 491524
  239.5 6.0 %copy-start.67 = (bf16[32]{0:T(256)(128)(2,1)S(1)}, bf16[32]{0:T(256)(128)(2,1)}, u32[]{:S(2)}) copy-start(bf16[32]{0:T(256)(128)(2,1)} %pad.24.clone) | copy-start | bytes 196
  242.0 5.2 %copy-start.9 = (bf16[2,4,4,2,2,40,128]{6,5,4,3,2,1,0:T(8,128)(2,1)S(1)}, bf16[2,4,4,2,2,40,128]{6,5,4,3,2,1,0:T(8,128)(2,1)}, u32[]{:S(2)}) copy-start(bf16[2,4,4,2,2,40,128]{6,5,4,3,2,1,0:T(8,128)(2,1)} %reshape_reshape.23.refs_0_) | copy-start | bytes 3932164
  (22 other events, 21.5 us)

commit v2 on v1

v2 whole, which is shorter than its diff:
```python
import functools
import math

import jax
import jax.numpy as jnp
from jax import lax
from jax.experimental import pallas as pl
from jax.experimental.pallas import tpu as pltpu
from jax.sharding import PartitionSpec as P

EPS = 1e-06
ROPE_BASE = 1000000.0
SCALE = 0.0625
EXP2_SCALE = SCALE * math.log2(math.e)
MESH = pl.DeviceIdType.MESH
BF16 = jnp.bfloat16
F32 = jnp.float32
ANY = pl.BlockSpec(memory_space=pl.ANY)
VMEM = pl.BlockSpec(memory_space=pltpu.VMEM)
HBM = pl.BlockSpec(memory_space=pltpu.HBM)
SMEM = pl.BlockSpec(memory_space=pltpu.SMEM)
NT = (((1,), (1,)), ((), ()))
TN = (((0,), (0,)), ((), ()))


def norm_scale(values, gain):
    return values * lax.rsqrt(jnp.mean(values * values, axis=-1, keepdims=True) + EPS) * gain


def place():
    c = lax.axis_index("ctx")
    h = lax.axis_index("fsdp")
    return h, c // 32, (c // 8) % 4, (c // 2) % 4, c % 2


def device(h, xl, z, y, core):
    return {"ctx": xl * 32 + z * 8 + y * 2 + core, "fsdp": h}


def axis_neighbour(axis, step):
    h, xl, z, y, core = place()
    if axis == "x":
        x = (2 * h + xl + step) % 4
        return device(x // 2, x % 2, z, y, core)
    if axis == "y":
        return device(h, xl, z, (y + step) % 4, core)
    return device(h, xl, (z + step) % 4, y, core)


def sibling():
    h, xl, z, y, core = place()
    return device(h, xl, z, y, 1 - core)


def greet(devices):
    barrier = pltpu.get_barrier_semaphore()
    for d in devices:
        pl.semaphore_signal(barrier, inc=1, device_id=d, device_id_type=MESH)
    pl.semaphore_wait(barrier, len(devices))


class Links:
    def __init__(self, send_sems, recv_sems):
        self.send_sems, self.recv_sems, self.count = send_sems, recv_sems, 0

    def send(self, src, dst, target):
        i = self.count
        self.count += 1
        assert i < self.send_sems.shape[0]
        copy = pltpu.make_async_remote_copy(
            src_ref=src,
            dst_ref=dst,
            send_sem=self.send_sems.at[i],
            recv_sem=self.recv_sems.at[i],
            device_id=target,
            device_id_type=MESH,
        )
        copy.start()
        return copy


class GatherRing:
    def __init__(self, links, axis, me, items):
        self.links, self.items = links, items
        self.me, self.left, self.right = me, (me + 3) % 4, (me + 1) % 4
        self.to_left, self.to_right = axis_neighbour(axis, 3), axis_neighbour(axis, 1)

    def start(self):
        self.first = []
        for whole, half in self.items:
            mine = whole(self.me)
            self.first.append(
                (
                    self.links.send(mine, mine, self.to_right),
                    self.links.send(mine, mine, self.to_left),
                )
            )

    def relay(self):
        self.second = []
        for (whole, half), (a, b) in zip(self.items, self.first):
            a.wait_recv()
            piece = half(self.left, 0)
            c = self.links.send(piece, piece, self.to_right)
            b.wait_recv()
            piece = half(self.right, 1)
            d = self.links.send(piece, piece, self.to_left)
            self.second.append((c, d))

    def finish(self):
        for c, d in self.second:
            c.wait_recv()
            d.wait_recv()

    def drain(self):
        for pair in self.first + self.second:
            for copy in pair:
                copy.wait_send()


def ring_of(links, axis, me, *items):
    ring = GatherRing(links, axis, me, items)
    ring.start()
    return ring


class PairGather:
    def __init__(self, links, axis, me, axis2, me2, piece, swap):
        self.links, self.axis, self.me, self.axis2, self.me2 = links, axis, me, axis2, me2
        self.piece, self.swap = piece, swap
        self.firsts, self.seconds = [], []

    def half(self, ref, k):
        return ref.at[pl.ds(64 * k, 64)]

    def spread(self, p, i):
        here = lambda j: self.piece(p, i, j)
        ring = ring_of(
            self.links, self.axis2, self.me2, (here, lambda j, k: self.half(here(j), k))
        )
        self.swap(here(self.me2))
        self.seconds.append((ring, here))

    def begin(self, p):
        here = lambda i: self.piece(p, i, self.me2)
        self.firsts.append(
            ring_of(self.links, self.axis, self.me, (here, lambda i, k: self.half(here(i), k)))
        )
        self.spread(p, self.me)

    def middle(self, p):
        ring = self.firsts[0 if len(self.seconds) == 2 else 1]
        ring.relay()
        self.spread(p, (self.me + 3) % 4)
        self.spread(p, (self.me + 1) % 4)
        ring.finish()
        self.spread(p, (self.me + 2) % 4)

    def relay(self, k):
        ring, here = self.seconds[k]
        ring.relay()
        self.swap(here((self.me2 + 3) % 4))
        self.swap(here((self.me2 + 1) % 4))

    def finish(self, k):
        ring, here = self.seconds[k]
        ring.finish()
        self.swap(here((self.me2 + 2) % 4))

    def drain(self):
        for ring in self.firsts + [ring for ring, _ in self.seconds]:
            ring.drain()


def front_kernel(
    wq, wk, wv, wo, wg, wu, wd, inputs, gains, cosine, sine,
    oq, okv, oo, og, ou, od, k_all, v_all, act_out, query_lin_out, key_lin_out, query_out,
    send_sems, recv_sems, local_sems,
):
    h, xl, z, y, core = place()
    o = 1 - h
    cross = device(1 - h, 1 - xl, z, y, core)
    other = device(h, 1 - xl, z, y, core)
    locals_ = []
    for i, (src, dst) in enumerate(
        (
            (wq, oq.at[h]),
            (wk, okv.at[h, :, pl.ds(0, 256)]),
            (wv, okv.at[h, :, pl.ds(256, 256)]),
            (wg, og.at[h]),
            (wu, ou.at[h]),
            (wd, od.at[h]),
            (wo, oo.at[h]),
        )
    ):
        copy = pltpu.make_async_copy(src, dst, local_sems.at[i])
        copy.start()
        locals_.append(copy)
    greet(
        [cross, other, sibling()]
        + [axis_neighbour(a, s) for a in ("y", "z") for s in (1, 3)]
    )
    links = Links(send_sems, recv_sems)

    def rows(i, n):
        return pl.ds(pl.multiple_of(i * n, 16), n)

    def cols(start, n):
        return pl.ds(pl.multiple_of(start, 128), n)

    def piece_g(ref, yy, zz):
        return ref.at[rows(yy, 80), cols(core * 1024 + zz * 256, 256)]

    def piece_kv(ref, yy, zz):
        return ref.at[rows(yy, 80), cols(zz * 128, 128)]

    def piece_o(ref, yy, zz):
        return ref.at[rows((core * 4 + zz) * 4 + yy, 16)]

    for copy in locals_[:3]:
        copy.wait()
    crosses = [links.send(piece_kv(okv.at[h], y, z), piece_kv(okv.at[h], y, z), cross)]
    for copy in locals_[3:]:
        copy.wait()
    crosses += [
        links.send(piece(dst.at[h], y, z), piece(dst.at[h], y, z), cross)
        for dst, piece in ((og, piece_g), (oo, piece_o), (ou, piece_g))
    ]
    half_q = lambda ref: ref.at[:, cols(core * 512, 512)]
    half_d = lambda ref: ref.at[rows(core, 512)]
    direct_q = links.send(half_q(oq.at[h]), half_q(oq.at[h]), cross)
    g, u, q, d, w, kv = og.at[o], ou.at[o], oq.at[o], od.at[o], oo.at[o], okv.at[o]
    swaps = []

    def swap(piece):
        swaps.append(links.send(piece, piece, sibling()))

    crosses[0].wait_recv()
    kv1 = ring_of(
        links, "z", z,
        (
            lambda i: piece_kv(kv, y, i),
            lambda i, k: kv.at[
                pl.ds(pl.multiple_of(y * 80 + k * 48, 16), 32 if k else 48), cols(i * 128, 128)
            ],
        ),
    )
    for copy in crosses[1:3]:
        copy.wait_recv()
    a1 = ring_of(
        links, "y", y,
        (
            lambda i: piece_g(g, i, z),
            lambda i, k: g.at[rows(i, 80), cols(core * 1024 + z * 256 + k * 128, 128)],
        ),
        (
            lambda i: piece_o(w, i, z),
            lambda i, k: w.at[
                rows((core * 4 + z) * 4 + i, 16), pl.ds(384 * k, 256 if k else 384)
            ],
        ),
    )
    crosses[3].wait_recv()
    b1 = ring_of(
        links, "z", z,
        (
            lambda i: piece_g(u, y, i),
            lambda i, k: u.at[rows(y, 80), cols(core * 1024 + i * 256 + k * 128, 128)],
        ),
    )
    kv1.relay()
    a1.relay()
    b1.relay()
    kv1.finish()
    kv2 = ring_of(
        links, "y", y,
        (lambda i: kv.at[rows(i, 80)], lambda i, k: kv.at[rows(i, 80), pl.ds(256 * k, 256)]),
    )
    a1.finish()
    a2 = ring_of(
        links, "z", z,
        (
            lambda i: g.at[:, cols(core * 1024 + i * 256, 256)],
            lambda i, k: g.at[pl.ds(160 * k, 160), cols(core * 1024 + i * 256, 256)],
        ),
        (
            lambda i: w.at[rows(core * 4 + i, 64)],
            lambda i, k: w.at[rows((core * 4 + i) * 2 + k, 32)],
        ),
    )
    b1.finish()
    kv2.relay()
    b2 = ring_of(
        links, "y", y,
        (
            lambda i: u.at[rows(i, 80), cols(core * 1024, 1024)],
            lambda i, k: u.at[rows(i, 80), cols(core * 1024 + k * 512, 512)],
        ),
    )
    kv2.finish()

    states = inputs[...].astype(F32)
    act = norm_scale(states, gains[0:1]).astype(BF16)
    act_out[...] = act
    kv_lin = jnp.dot(act, okv[...].reshape(640, 512), preferred_element_type=F32)
    key_lin_out[...] = kv_lin[:, :256]
    cos, sin = cosine[...], sine[...]

    def turned(lin, gain):
        n = norm_scale(lin, gain)
        a, b = n[:, :128], n[:, 128:]
        return jnp.concatenate([a * cos - b * sin, b * cos + a * sin], axis=1).astype(BF16)

    k_all[xl, z, y, core] = turned(kv_lin[:, :256], gains[2:3, :256])
    v_all[xl, z, y, core] = kv_lin[:, 256:].astype(BF16)
    own = lambda ref: ref.at[xl, z, y, core]
    first = [links.send(own(ref), own(ref), other) for ref in (k_all, v_all)]
    keys = PairGather(links, "y", y, "z", z, lambda p, i, j: k_all.at[p, j, i, core], swap)
    values = PairGather(links, "z", z, "y", y, lambda p, i, j: v_all.at[p, i, j, core], swap)
    keys.begin(xl)
    values.begin(xl)
    direct_q.wait_recv()
    swap(half_q(q))
    swap_q = swaps.pop()
    direct_d = links.send(half_d(od.at[h]), half_d(od.at[h]), cross)
    a2.relay()
    b2.relay()
    for copy, gather in zip(first, (keys, values)):
        copy.wait_recv()
        gather.begin(1 - xl)
    swap_q.wait_recv()
    for head in range(4):
        lin = jnp.dot(
            act,
            oq[:, :, head * 256 : (head + 1) * 256].reshape(640, 256),
            preferred_element_type=F32,
        )
        query_lin_out[:, head * 256 : (head + 1) * 256] = lin
        row = turned(lin, gains[1:2, :256])
        query_out[head * 64 : (head + 1) * 64] = row[:64]
        query_out[256 + head * 64 : 256 + (head + 1) * 64] = row[64:]

    for gather in (keys, values):
        gather.middle(xl)
    for gather in (keys, values):
        gather.middle(1 - xl)
    a2.finish()
    b2.finish()
    swap(g.at[:, cols(core * 1024, 1024)])
    swap(u.at[:, cols(core * 1024, 1024)])
    swap(w.at[rows(core, 256)])
    direct_d.wait_recv()
    swap(half_d(d))
    for k in range(8):
        for gather in (keys, values):
            gather.relay(k)
    for k in range(8):
        for gather in (keys, values):
            gather.finish(k)
    for ring in (kv1, kv2, a1, b1, a2, b2, keys, values):
        ring.drain()
    for copy in crosses + [direct_q, direct_d, swap_q] + first:
        copy.wait_send()
    for copy in swaps:
        copy.wait()


def front(weights, inputs, gains, cosine, sine):
    wq, wk, wv, wo, wg, wu, wd = weights
    full = lambda rows, width: pltpu.VMEM((2, rows, width), BF16)
    kv = pltpu.VMEM((2, 4, 4, 2, 128, 256), BF16)
    count = 4 + 2 + 2 + 4 * (2 + 4 + 2) + 2 * (2 + 8) * 4 + 2 * 8 * 4 + 5
    outs = pl.pallas_call(
        front_kernel,
        name="front",
        out_shape=(
            full(320, 1024), full(320, 512), full(512, 640), full(320, 2048), full(320, 2048),
            full(1024, 640), kv, kv,
            jax.ShapeDtypeStruct((128, 640), BF16),
            jax.ShapeDtypeStruct((128, 1024), F32),
            jax.ShapeDtypeStruct((128, 256), F32),
            jax.ShapeDtypeStruct((512, 256), BF16),
        ),
        in_specs=[HBM] * 7 + [VMEM] * 4,
        out_specs=(VMEM,) * 12,
        scratch_shapes=[
            pltpu.SemaphoreType.DMA((count,)),
            pltpu.SemaphoreType.DMA((count,)),
            pltpu.SemaphoreType.DMA((7,)),
        ],
        compiler_params=pltpu.CompilerParams(
            collective_id=1, has_side_effects=True, vmem_limit_bytes=16 << 20
        ),
    )(*[pltpu.with_memory_space_constraint(w, pltpu.HBM) for w in weights], inputs, gains, cosine, sine)
    flat = [o.reshape(2 * o.shape[1], o.shape[2]) for o in outs[:6]]
    return flat + [o.reshape(64, 128, 256) for o in outs[6:8]] + list(outs[8:])


def add_into(dst, src):
    dst[...] = dst[...] + src[...]


def sum_into(dst, terms):
    total = terms[0][...].astype(dst.dtype)
    for t in terms[1:]:
        total = total + t[...].astype(dst.dtype)
    dst[...] = total


class SumRing:
    def __init__(self, links, axis, me, block, half, pass0, pass1, from_left, from_right, part):
        self.links = links
        self.me, self.left, self.right, self.far = me, (me + 3) % 4, (me + 1) % 4, (me + 2) % 4
        self.to_left, self.to_right = axis_neighbour(axis, 3), axis_neighbour(axis, 1)
        self.block, self.half = block, half
        self.pass0, self.pass1 = pass0, pass1
        self.from_left, self.from_right = from_left, from_right
        self.part = part

    def start(self, ready):
        send = self.links.send
        ready(self.far)
        self.a = send(self.half(self.far, 0), self.pass0, self.to_right)
        self.b = send(self.half(self.far, 1), self.pass1, self.to_left)
        ready(self.right)
        self.c = send(self.half(self.right, 1), self.part(self.from_left, 1), self.to_right)
        ready(self.left)
        self.d = send(self.half(self.left, 0), self.part(self.from_right, 0), self.to_left)
        ready(self.me)

    def relay(self):
        send = self.links.send
        self.a.wait_recv()
        add_into(self.half(self.right, 0), self.pass0)
        self.e = send(self.half(self.right, 0), self.part(self.from_left, 0), self.to_right)
        self.b.wait_recv()
        add_into(self.half(self.left, 1), self.pass1)
        self.f = send(self.half(self.left, 1), self.part(self.from_right, 1), self.to_left)

    def finish(self, out):
        for copy in (self.c, self.d, self.e, self.f):
            copy.wait_recv()
        sum_into(out, [self.block(self.me), self.from_left, self.from_right])

    def drain(self):
        for copy in (self.a, self.b, self.c, self.d, self.e, self.f):
            copy.wait_send()


class Direct:
    def __init__(self, links, axis, me, block, got):
        self.links, self.axis, self.me, self.block, self.got = links, axis, me, block, got

    def start(self):
        self.copies = [
            self.links.send(
                self.block((self.me + step) % 4), self.got.at[step - 1], axis_neighbour(self.axis, step)
            )
            for step in (1, 2, 3)
        ]

    def finish(self, out):
        for copy in self.copies:
            copy.wait_recv()
        sum_into(out, [self.block(self.me)] + [self.got.at[i] for i in range(3)])

    def drain(self):
        for copy in self.copies:
            copy.wait_send()


def nothing(i):
    pass


class KeySum:
    SCRATCH = 12

    def __init__(self, links, source, out, scratch, axes):
        h, xl, z, y, core = place()
        self.links, self.source, self.out, self.axes = links, source, out, axes
        self.xl, self.core, self.me = xl, core, {"y": y, "z": z}
        self.got, self.p0, self.p1, self.fl, self.fr, self.second, self.q0, self.q1, self.gl, self.gr, self.third, self.last = scratch
        self.other = device(h, 1 - xl, z, y, core)

    @staticmethod
    def scratch():
        buf = lambda *lead: pltpu.VMEM(lead + (128, 256), BF16)
        return [buf(2, 4, 4), buf(4), buf(4), buf(2, 4), buf(2, 4), buf(2, 4), buf(), buf(), buf(2), buf(2), buf(2), buf()]

    def at(self, ref, i, *more):
        return ref.at[(slice(None), i, slice(None)) + more] if self.axes[0] == "z" else ref.at[(slice(None), slice(None), i) + more]

    def swap(self):
        me = self.me[self.axes[0]]
        self.swaps = [
            self.links.send(self.at(self.source, i, 1 - self.core), self.at(self.got, i), sibling())
            for i in ((me + 2) % 4, (me + 1) % 4, (me + 3) % 4, me)
        ]
        self.pending = list(self.swaps)

    def ready(self, i):
        self.pending.pop(0).wait_recv()
        mine, got = self.at(self.source, i, self.core), self.at(self.got, i)
        add_into(got, mine)

    def start(self):
        first, second = self.axes
        half = lambda i, k: self.got.at[(k, i) if first == "z" else (k, slice(None), i)]
        self.ring = SumRing(
            self.links, first, self.me[first], lambda i: self.at(self.got, i), half,
            self.p0, self.p1, self.fl, self.fr, lambda ref, k: ref.at[k],
        )
        self.ring2 = SumRing(
            self.links, second, self.me[second], lambda i: self.second.at[:, i],
            lambda i, k: self.second.at[k, i],
            self.q0, self.q1, self.gl, self.gr, lambda ref, k: ref.at[k],
        )
        self.ring.start(self.ready)

    def relay(self):
        self.ring.relay()

    def next(self):
        self.ring.finish(self.second)
        self.ring2.start(nothing)

    def relay2(self):
        self.ring2.relay()

    def next2(self):
        self.ring2.finish(self.third)
        self.copy = self.links.send(self.third.at[1 - self.xl], self.last, self.other)

    def finish(self):
        self.copy.wait_recv()
        self.out[...] = self.third[self.xl].astype(F32) + self.last[...].astype(F32)

    def drain(self):
        self.ring.drain()
        self.ring2.drain()
        for copy in self.swaps + [self.copy]:
            copy.wait_send()


SIZES = {"xl": 2, "z": 4, "y": 4, "xh": 2}


def pick(ref, dims, axis, i, core=None):
    spot, left = [], []
    for name in dims:
        if axis == "x" and name == "xl":
            spot.append(i % 2)
        elif axis == "x" and name == "xh":
            spot.append(i // 2)
        elif name == axis:
            spot.append(i)
        else:
            spot.append(slice(None))
            left.append(name)
        if core is not None and name == "y":
            spot.append(core)
    return ref.at[tuple(spot)], tuple(left)


def without(dims, axis):
    return tuple(n for n in dims if not n.startswith(axis))


def sizes(dims):
    return tuple(SIZES[n] for n in dims)


def first_half(ref, k):
    n = ref.shape[0] // 2
    return ref.at[pl.ds(n * k, n)]


class WeightSum:
    SCRATCH = 12
    DIMS = ("xl", "z", "y", "xh")

    def __init__(self, links, source, out, scratch, axes):
        h, xl, z, y, core = place()
        self.links, self.source, self.out, self.axes = links, source, out, axes
        self.core, self.me = core, {"x": 2 * h + xl, "y": y, "z": z}
        (
            self.got, self.p0, self.p1, self.fl, self.fr,
            self.total2, self.q0, self.q1, self.gl, self.gr, self.total3, self.last,
        ) = scratch
        self.dims2 = without(self.DIMS, axes[0])
        self.dims3 = without(self.dims2, axes[1])

    @classmethod
    def scratch(cls, rows, axes):
        buf = lambda *lead: pltpu.VMEM(lead + (rows, 128), BF16)
        two = without(cls.DIMS, axes[0])
        three = without(two, axes[1])
        a, b = sizes(two), sizes(three)
        half_a, half_b = (a[0] // 2,) + a[1:], (b[0] // 2,) + b[1:]
        return (
            [buf(*sizes(cls.DIMS)), buf(*half_a), buf(*half_a), buf(*a), buf(*a)]
            + [buf(*a), buf(*half_b), buf(*half_b), buf(*b), buf(*b)]
            + [buf(*b), buf(3)]
        )

    def mine(self, i, core):
        return pick(self.source, self.DIMS, self.axes[0], i, core)[0]

    def block(self, i):
        return pick(self.got, self.DIMS, self.axes[0], i)[0]

    def block2(self, i):
        return pick(self.total2, self.dims2, self.axes[1], i)[0]

    def block3(self, i):
        return pick(self.total3, self.dims3, self.axes[2], i)[0]

    def swap(self):
        me = self.me[self.axes[0]]
        self.swaps = [
            self.links.send(self.mine(i, 1 - self.core), self.block(i), sibling())
            for i in ((me + 2) % 4, (me + 1) % 4, (me + 3) % 4, me)
        ]
        self.pending = list(self.swaps)

    def ready(self, i):
        self.pending.pop(0).wait_recv()
        add_into(self.block(i), self.mine(i, self.core))

    def start(self):
        first, second, third = self.axes
        self.ring = SumRing(
            self.links, first, self.me[first], self.block,
            lambda i, k: first_half(self.block(i), k),
            self.p0, self.p1, self.fl, self.fr, first_half,
        )
        self.ring2 = SumRing(
            self.links, second, self.me[second], self.block2,
            lambda i, k: first_half(self.block2(i), k),
            self.q0, self.q1, self.gl, self.gr, first_half,
        )
        self.direct = Direct(self.links, third, self.me[third], self.block3, self.last)
        self.ring.start(self.ready)

    def relay(self):
        self.ring.relay()

    def next(self):
        self.ring.finish(self.total2)
        self.ring2.start(nothing)

    def relay2(self):
        self.ring2.relay()

    def next2(self):
        self.ring2.finish(self.total3)
        self.direct.start()

    def finish(self):
        self.direct.finish(self.out)

    def drain(self):
        self.ring.drain()
        self.ring2.drain()
        self.direct.drain()
        for copy in self.swaps:
            copy.wait_send()


def tile(ref, inverse, step):
    parts = []
    for j in range(8):
        block = step * 8 + j
        late = block >= 64
        owner = inverse[jnp.where(late, 127 - block, block)]
        half = pl.multiple_of(jnp.where(late, 64, 0), 64)
        parts.append(ref[owner, pl.ds(half, 64), :])
    return jnp.concatenate(parts, axis=0)


def attend(own, inverse, query, keys, values, acc, weight):
    acc[...] = jnp.zeros_like(acc)
    weight[...] = jnp.zeros_like(weight)

    def step_for(part, block, step, masked):
        here = pl.ds(part * 256, 256)
        k = tile(keys, inverse, step)
        v = tile(values, inverse, step)
        raw = lax.dot_general(query[here, :], k, NT, preferred_element_type=F32)
        p = jnp.exp2(raw * EXP2_SCALE)
        if masked:
            token = lax.broadcasted_iota(jnp.int32, (256, 512), 0) % 64 + block * 64
            position = lax.broadcasted_iota(jnp.int32, (256, 512), 1) + step * 512
            p = jnp.where(position <= token, p, 0.0)
        weight[here, :] += p[:, :128] + p[:, 128:256] + p[:, 256:384] + p[:, 384:]
        acc[here, :] += jnp.dot(p.astype(BF16), v, preferred_element_type=F32)

    for part in range(2):
        block = own if part == 0 else 127 - own
        full = block // 8

        @pl.loop(0, full)
        def _(step):
            step_for(part, block, step, False)

        step_for(part, block, full, True)


def attend_back(own, inverse, query, d_out, log_sum, delta, keys, values, d_query, d_keys, d_values):
    d_query[...] = jnp.zeros_like(d_query)

    def terms(part, step, k, v, masked):
        rows = pl.ds(part * 256, 256)
        block = own if part == 0 else 127 - own
        q = query[rows, :]
        g = d_out[rows, :]
        raw = lax.dot_general(k, q, NT, preferred_element_type=F32)
        p = jnp.exp2(raw * EXP2_SCALE - log_sum[:, part * 256 : (part + 1) * 256])
        if masked:
            position = lax.broadcasted_iota(jnp.int32, (512, 256), 0) + step * 512
            token = lax.broadcasted_iota(jnp.int32, (512, 256), 1) % 64 + block * 64
            p = jnp.where(position <= token, p, 0.0)
        d_p = lax.dot_general(v, g, NT, preferred_element_type=F32)
        d_s = (p * (d_p - delta[:, part * 256 : (part + 1) * 256])).astype(BF16)
        d_query[rows, :] += lax.dot_general(d_s, k, TN, preferred_element_type=F32)
        d_k = jnp.dot(d_s, q, preferred_element_type=F32)
        d_v = jnp.dot(p.astype(BF16), g, preferred_element_type=F32)
        return d_k, d_v

    def store(step, d_k, d_v):
        for j in range(8):
            block = step * 8 + j
            late = block >= 64
            owner = inverse[jnp.where(late, 127 - block, block)]
            half = pl.multiple_of(jnp.where(late, 64, 0), 64)
            d_keys[owner, pl.ds(half, 64), :] = (d_k[j * 64 : (j + 1) * 64] * SCALE).astype(BF16)
            d_values[owner, pl.ds(half, 64), :] = d_v[j * 64 : (j + 1) * 64].astype(BF16)

    early_full = own // 8
    late_full = (127 - own) // 8

    @pl.loop(0, early_full)
    def _(step):
        k = tile(keys, inverse, step)
        v = tile(values, inverse, step)
        d_k, d_v = terms(1, step, k, v, False)
        d_k2, d_v2 = terms(0, step, k, v, False)
        store(step, d_k + d_k2, d_v + d_v2)

    k = tile(keys, inverse, early_full)
    v = tile(values, inverse, early_full)
    d_k, d_v = terms(1, early_full, k, v, False)
    d_k2, d_v2 = terms(0, early_full, k, v, True)
    store(early_full, d_k + d_k2, d_v + d_v2)

    @pl.loop(early_full + 1, late_full)
    def _(step):
        d_k, d_v = terms(1, step, tile(keys, inverse, step), tile(values, inverse, step), False)
        store(step, d_k, d_v)

    d_k, d_v = terms(
        1, late_full, tile(keys, inverse, late_full), tile(values, inverse, late_full), True
    )
    store(late_full, d_k, d_v)
    zero = jnp.zeros((512, 256), F32)

    @pl.loop(late_full + 1, 16)
    def _(step):
        store(step, zero, zero)

    d_query[...] = d_query[...] * SCALE


def dot(a, b):
    return jnp.dot(a, b, preferred_element_type=F32)


def dot_nt(a, b):
    return lax.dot_general(a, b, NT, preferred_element_type=F32)


def dot_tn(a, b):
    return lax.dot_general(a, b, TN, preferred_element_type=F32)


def norm_back(values, gain, d_out):
    r = lax.rsqrt(jnp.mean(values * values, axis=-1, keepdims=True) + EPS)
    n = values * r
    d_gain = jnp.sum(d_out * n, axis=0, keepdims=True)
    d_n = d_out * gain
    return r * (d_n - n * jnp.mean(d_n * n, axis=-1, keepdims=True)), d_gain


def gelu_terms(x):
    c = math.sqrt(2.0 / math.pi)
    square = x * x
    t = jnp.tanh(c * x * (1.0 + 0.044715 * square))
    half = 0.5 * (1.0 + t)
    slope = half + 0.5 * x * (1.0 - t * t) * c * (1.0 + 3 * 0.044715 * square)
    return x * half, slope


def by_fives(act):
    i = lax.broadcasted_iota(jnp.int32, (640, 640), 0)
    j = lax.broadcasted_iota(jnp.int32, (640, 640), 1)
    chosen = (i == 5 * (j % 128) + j // 128).astype(F32).astype(BF16)
    return dot(act, chosen).astype(BF16)


def spread_rows(flat, act, grad, rows, first=0):
    tiles = grad.shape[1] // 128
    for t in range(5):
        part = dot_tn(act[:, t * 128 : (t + 1) * 128], grad)
        for c in range(tiles):
            flat[pl.ds(first + t * tiles + c, 128, stride=rows), :] = part[
                :, c * 128 : (c + 1) * 128
            ]


def pack(out, flat, rows):
    @pl.loop(0, 128)
    def _(i):
        out[i] = flat[pl.ds(pl.multiple_of(i * rows, 8), rows), :].astype(BF16)


def middle_kernel(
    inverse, pair, query, keys, values, inputs, cotangent, wo, wg, wu, wd, gains,
    layer_out, grad_resid_out, d_query, d_keys, d_values, gr_down, gr_gate, gr_up, gr_out, gr_gains,
    acc, weight, gate, upper, hidden, d_gate, d_upper, att, d_att_rows, flat,
):
    own = pair[0]
    attend(own, inverse, query, keys, values, acc, weight)
    attended = acc[...] / jnp.sum(weight[...], axis=1, keepdims=True)
    acc[...] = attended
    ones = jnp.ones((8, 128), F32)
    sums = lax.dot_general(
        ones, weight[...], NT, precision=lax.Precision.HIGHEST, preferred_element_type=F32
    )
    log_sum = jnp.log2(sums[:1])
    attended = attended.astype(BF16)
    for b in range(2):
        for head in range(4):
            att[b * 64 : (b + 1) * 64, head * 256 : (head + 1) * 256] = attended[
                b * 256 + head * 64 : b * 256 + (head + 1) * 64
            ]

    att_lin = dot(att[...], wo[...])
    resid = inputs[...].astype(F32) + norm_scale(att_lin, gains[3:4])
    act_two = norm_scale(resid, gains[4:5]).astype(BF16)
    for c in range(4):
        s = slice(c * 512, (c + 1) * 512)
        gate[:, s] = dot(act_two, wg[:, s])
        upper[:, s] = dot(act_two, wu[:, s])
        hidden[:, s] = (gelu_terms(gate[:, s])[0] * upper[:, s]).astype(BF16)
    down = dot(hidden[...], wd[...])
    layer_out[...] = (resid + norm_scale(down, gains[5:6])).astype(BF16)

    grad_y = cotangent[...].astype(F32)
    d_down, d_post_ff = norm_back(down, gains[5:6], grad_y)
    d_down = d_down.astype(BF16)
    d_act_two = jnp.zeros((128, 640), F32)
    for c in range(4):
        s = slice(c * 512, (c + 1) * 512)
        d_hidden = dot_nt(d_down, wd[s, :])
        value, slope = gelu_terms(gate[:, s])
        a = (d_hidden * upper[:, s] * slope).astype(BF16)
        b = (d_hidden * value).astype(BF16)
        d_gate[:, s] = a
        d_upper[:, s] = b
        d_act_two = d_act_two + dot_nt(a, wg[:, s]) + dot_nt(b, wu[:, s])
    d_resid, d_pre_ff = norm_back(resid, gains[4:5], d_act_two)
    grad_resid = grad_y + d_resid
    grad_resid_out[...] = grad_resid
    d_att, d_post_attn = norm_back(att_lin, gains[3:4], grad_resid)
    d_att = d_att.astype(BF16)
    gr_gains[...] = jnp.concatenate(
        [d_post_attn, d_pre_ff, d_post_ff, jnp.zeros((5, 640), F32)], axis=0
    )
    d_attended = dot_nt(d_att, wo[...]).astype(BF16)
    for b in range(2):
        for head in range(4):
            d_att_rows[b * 256 + head * 64 : b * 256 + (head + 1) * 64] = d_attended[
                b * 64 : (b + 1) * 64, head * 256 : (head + 1) * 256
            ]
    delta = lax.dot_general(
        jnp.ones((8, 256), F32),
        d_att_rows[...].astype(F32) * acc[...],
        NT,
        precision=lax.Precision.HIGHEST,
        preferred_element_type=F32,
    )[:1]

    @pl.loop(0, 16)
    def _(i):
        part = dot_tn(hidden[:, pl.ds(pl.multiple_of(i * 128, 128), 128)], d_down).astype(BF16)
        for j in range(8):
            for c in range(5):
                gr_down[i * 8 + j, c * 16 : (c + 1) * 16, :] = part[
                    j * 16 : (j + 1) * 16, c * 128 : (c + 1) * 128
                ]

    @pl.loop(0, 8)
    def _(i):
        part = dot_tn(att[:, pl.ds(pl.multiple_of(i * 128, 128), 128)], d_att)
        for j in range(16):
            rows = part[j * 8 : (j + 1) * 8]
            gr_out[i * 16 + j] = jnp.concatenate(
                [rows[:, c * 128 : (c + 1) * 128] for c in range(5)], axis=0
            ).astype(BF16)

    fives = by_fives(act_two)
    spread_rows(flat, fives, d_gate[...], 80)
    pack(gr_gate, flat, 80)
    spread_rows(flat, fives, d_upper[...], 80)
    pack(gr_up, flat, 80)

    attend_back(
        own, inverse, query, d_att_rows, log_sum, delta, keys, values, d_query, d_keys, d_values
    )


def middle(*args):
    block = lambda rows: pltpu.VMEM((128, rows, 128), BF16)
    kv = pltpu.VMEM((64, 128, 256), BF16)
    return pl.pallas_call(
        middle_kernel,
        name="middle",
        out_shape=(
            jax.ShapeDtypeStruct((128, 640), BF16),
            jax.ShapeDtypeStruct((128, 640), F32),
            jax.ShapeDtypeStruct((512, 256), F32),
            kv, kv, block(80), block(80), block(80), block(40),
            jax.ShapeDtypeStruct((8, 640), F32),
        ),
        in_specs=[SMEM, SMEM] + [VMEM] * 10,
        out_specs=(VMEM,) * 10,
        scratch_shapes=[
            pltpu.VMEM((512, 256), F32),
            pltpu.VMEM((512, 128), F32),
            pltpu.VMEM((128, 2048), F32),
            pltpu.VMEM((128, 2048), F32),
            pltpu.VMEM((128, 2048), BF16),
            pltpu.VMEM((128, 2048), BF16),
            pltpu.VMEM((128, 2048), BF16),
            pltpu.VMEM((128, 1024), BF16),
            pltpu.VMEM((512, 256), BF16),
            pltpu.VMEM((128 * 80, 128), F32),
        ],
        compiler_params=pltpu.CompilerParams(vmem_limit_bytes=23 << 20),
    )(*args)


FIRST_ROWS, FIRST_ORDERS = (80, 80, 80, 40), ("xyz", "xzy", "yzx", "zxy")
LAST_ROWS, LAST_ORDERS = (40, 32), ("xyz", "yzx")


def pack_places(out, flat, rows):
    @pl.loop(0, 128)
    def _(i):
        out[i // 64, (i // 16) % 4, (i // 4) % 4, (i // 2) % 2, i % 2] = flat[
            pl.ds(pl.multiple_of(i * rows, 8), rows), :
        ].astype(BF16)


def project_back(
    d_query, d_key, d_value, query_lin, key_lin, act_one, inputs, wq, wkv, gains, cosine, sine, grad_resid, d_gains,
    input_grad, gr_query, gr_tail,
    d_query_lin, d_kv_lin, flat, flat_tail,
):
    cos, sin = cosine[...], sine[...]

    def turn_back(lin, gain, grad):
        a, b = grad[:, :128], grad[:, 128:]
        d_n = jnp.concatenate([a * cos + b * sin, b * cos - a * sin], axis=1)
        return norm_back(lin, gain, d_n)

    fives = by_fives(act_one[...])
    d_gain_query = jnp.zeros((1, 256), F32)
    for head in range(4):
        cut = slice(head * 256, (head + 1) * 256)
        grad = jnp.concatenate(
            [d_query[b * 256 + head * 64 : b * 256 + (head + 1) * 64] for b in range(2)], axis=0
        )
        d_lin, d_gain = turn_back(query_lin[:, cut], gains[1:2, :256], grad)
        d_query_lin[:, cut] = d_lin.astype(BF16)
        d_gain_query = d_gain_query + d_gain
    spread_rows(flat, fives, d_query_lin[...], 40)
    pack_places(gr_query, flat, 40)
    d_act = dot_nt(d_query_lin[...], wq[...])
    yield
    d_lin, d_gain_key = turn_back(key_lin[...], gains[2:3, :256], d_key[...])
    d_kv_lin[:, :256] = d_lin.astype(BF16)
    d_kv_lin[:, 256:] = d_value[...].astype(BF16)
    d_act = d_act + dot_nt(d_kv_lin[...], wkv[...])
    d_states, d_gain_in = norm_back(inputs[...].astype(F32), gains[0:1], d_act)
    input_grad[...] = (grad_resid[...] + d_states).astype(BF16)
    flat_tail[...] = jnp.zeros_like(flat_tail)
    spread_rows(flat_tail, fives, d_kv_lin[...], 32)
    total = jnp.zeros((128, 128), F32)
    column = 0
    for row, each in (
        (d_gain_in, 5),
        (d_gains[0:1], 5),
        (d_gains[1:2], 5),
        (d_gains[2:3], 5),
        (d_gain_query, 2),
        (d_gain_key, 2),
    ):
        n = 128 * each
        owner = lax.broadcasted_iota(jnp.int32, (128, n), 1) // each
        mine = owner == lax.broadcasted_iota(jnp.int32, (128, n), 0)
        spot = lax.broadcasted_iota(jnp.int32, (n, 128), 0) % each + column
        here = spot == lax.broadcasted_iota(jnp.int32, (n, 128), 1)
        total = total + dot(
            jnp.where(mine, row, 0.0).astype(BF16), here.astype(F32).astype(BF16)
        )
        column += each
    flat_tail[pl.ds(20, 128, stride=32), :] = total
    pack_places(gr_tail, flat_tail, 32)
    yield


def back_kernel(*refs):
    refs = list(refs)

    def take(n):
        some = refs[:n]
        del refs[:n]
        return some

    kv_sources, first_sources, others = take(2), take(4), take(12)
    input_grad, o_query, o_key, o_value, o_output, o_gate, o_up, o_down, o_gains = take(9)
    kv_sums = take(2)
    first_sums, last_sources, last_sums, temps = take(4), take(2), take(2), take(4)
    kv_scratch = [take(KeySum.SCRATCH) for _ in range(2)]
    first_scratch = [take(WeightSum.SCRATCH) for _ in range(4)]
    last_scratch = [take(WeightSum.SCRATCH) for _ in range(2)]
    send_sems, recv_sems = refs
    greet(
        [sibling()] + [axis_neighbour(a, s) for a in ("x", "y", "z") for s in (1, 2, 3)]
    )
    links = Links(send_sems, recv_sems)
    kv = [
        KeySum(links, *args)
        for args in zip(kv_sources, kv_sums, kv_scratch, ("zy", "yz"))
    ]
    first = [
        WeightSum(links, *args)
        for args in zip(first_sources, first_sums, first_scratch, FIRST_ORDERS)
    ]
    final = [
        WeightSum(links, *args)
        for args in zip(last_sources, last_sums, last_scratch, LAST_ORDERS)
    ]

    def run(group, *stages):
        for stage in stages:
            for s in group:
                getattr(s, stage)()

    d_query, query_lin = others[:2]
    projections = project_back(
        d_query, *kv_sums, *others[1:], input_grad, *last_sources, *temps
    )
    run(kv, "swap")
    run(first, "swap")
    run(kv, "start")
    run(first, "start")
    next(projections)
    run(kv, "relay")
    run(first, "relay")
    run(kv, "next", "relay2", "next2")
    run(first, "next")
    run(kv, "finish")
    next(projections)
    run(final, "swap", "start")
    run(first, "relay2", "next2")
    run(final, "relay", "next", "relay2", "next2")
    run(first, "finish")
    run(final, "finish")
    run(kv + first + final, "drain")

    s_down, s_gate, s_up, s_output = first_sums
    s_query, s_tail = last_sums
    for c in range(5):
        cut = slice(c * 128, (c + 1) * 128)
        o_down[:, cut] = s_down[c * 16 : (c + 1) * 16, :]
        o_output[:, cut] = s_output[c * 8 : (c + 1) * 8, :]
    for out, source, first_row, step, tiles in (
        (o_gate, s_gate, 0, 16, 16),
        (o_up, s_up, 0, 16, 16),
        (o_query, s_query, 0, 8, 8),
        (o_key, s_tail, 0, 4, 2),
        (o_value, s_tail, 2, 4, 2),
    ):
        for c in range(tiles):
            out[:, c * 128 : (c + 1) * 128] = source[pl.ds(first_row + c, 5, stride=step), :]
    o_gains[...] = s_tail[20:21, :]


def back(kv, grads, others):
    buf = lambda *shape: pltpu.VMEM(shape, F32)
    scratch = [buf(128, 256)] * 2
    scratch += [buf(rows, 128) for rows in FIRST_ROWS]
    scratch += [pltpu.VMEM((2, 4, 4, 2, 2, rows, 128), BF16) for rows in LAST_ROWS]
    scratch += [buf(rows, 128) for rows in LAST_ROWS]
    scratch += [
        pltpu.VMEM((128, 1024), BF16),
        pltpu.VMEM((128, 512), BF16),
        buf(128 * 40, 128),
        buf(128 * 32, 128),
    ]
    for _ in kv:
        scratch += KeySum.scratch()
    for rows, order in zip(FIRST_ROWS + LAST_ROWS, FIRST_ORDERS + LAST_ORDERS):
        scratch += WeightSum.scratch(rows, order)
    count = 2 * 17 + 6 * 19
    out = lambda rows, width: jax.ShapeDtypeStruct((rows, width), F32)
    return pl.pallas_call(
        back_kernel,
        name="back",
        out_shape=(
            jax.ShapeDtypeStruct((128, 640), BF16),
            out(5, 1024), out(5, 256), out(5, 256), out(8, 640), out(5, 2048), out(5, 2048),
            out(16, 640), out(1, 128),
        ),
        in_specs=[VMEM] * 18,
        out_specs=(VMEM,) * 9,
        scratch_shapes=scratch
        + [pltpu.SemaphoreType.DMA((count,)), pltpu.SemaphoreType.DMA((count,))],
        compiler_params=pltpu.CompilerParams(
            collective_id=2, has_side_effects=True, vmem_limit_bytes=36 << 20
        ),
    )(
        *[g.reshape((2, 4, 4, 2) + g.shape[1:]) for g in kv],
        *[g.reshape((2, 4, 4, 2, 2) + g.shape[1:]) for g in grads],
        *others,
    )


def local(
    inputs,
    pair_order,
    w_query,
    w_key,
    w_value,
    w_output,
    w_gate,
    w_up,
    w_down,
    gain_in,
    gain_query,
    gain_key,
    gain_post_attn,
    gain_pre_ff,
    gain_post_ff,
    cotangent,
):
    rows = 128
    me_index = lax.axis_index("ctx")
    own_pair = lax.dynamic_slice_in_dim(pair_order, me_index, 1)
    within = jnp.arange(rows, dtype=jnp.int32)
    block_id = jnp.where(within < 64, own_pair, 127 - own_pair)
    positions = block_id * 64 + within % 64
    freq = ROPE_BASE ** (-jnp.arange(128, dtype=F32) / 128)
    angles = positions.astype(F32)[:, None] * freq
    cosine, sine = jnp.cos(angles), jnp.sin(angles)
    matches = pair_order[None, :] == jnp.arange(64, dtype=jnp.int32)[:, None]
    inverse = jnp.sum(jnp.where(matches, jnp.arange(64, dtype=jnp.int32)[None, :], 0), axis=1)
    wide = lambda g: jnp.pad(g, (0, 640 - g.shape[0]))
    gains = jnp.stack(
        [wide(g) for g in (gain_in, gain_query, gain_key, gain_post_attn, gain_pre_ff, gain_post_ff)]
        + [jnp.zeros((640,), F32)] * 2
    )
    (
        wq_all, wkv_all, wo_all, wg_all, wu_all, wd_all, keys, values,
        act_one, query_lin, key_lin, query,
    ) = front(
        (w_query, w_key, w_value, w_output, w_gate, w_up, w_down), inputs[0], gains, cosine, sine
    )
    layer_out, grad_resid, d_query, d_keys, d_values, gr_down, gr_gate, gr_up, gr_out, d_gains = middle(
        inverse, own_pair, query, keys, values, inputs[0], cotangent[0],
        wo_all, wg_all, wu_all, wd_all, gains,
    )
    input_grad, s_query, s_key, s_value, s_output, s_gate, s_up, s_down, s_gains = back(
        (d_keys, d_values), (gr_down, gr_gate, gr_up, gr_out),
        (d_query, query_lin, key_lin, act_one, inputs[0], wq_all, wkv_all, gains, cosine, sine, grad_resid, d_gains),
    )
    s_gains = s_gains[0]
    return (
        layer_out[None],
        input_grad[None],
        s_query,
        s_key,
        s_value,
        s_output,
        s_gate,
        s_up,
        s_down,
        s_gains[0:5],
        s_gains[20:22],
        s_gains[22:24],
        s_gains[5:10],
        s_gains[10:15],
        s_gains[15:20],
    )


def solution(mesh):
    placed = (
        P("fsdp", "ctx", None),
        P(),
        P("fsdp", None),
        P("fsdp", None),
        P("fsdp", None),
        P("fsdp", None),
        P("fsdp", None),
        P("fsdp", None),
        P("fsdp", None),
        P(),
        P(),
        P(),
        P(),
        P(),
        P(),
        P("fsdp", "ctx", None),
    )
    both = ("ctx", "fsdp")
    return jax.shard_map(
        local,
        mesh=mesh,
        in_specs=placed,
        out_specs=(P("fsdp", "ctx", None),) * 2 + (P(both, None),) * 7 + (P(both),) * 6,
        check_vma=False,
    )
```

time: 274 us -> 204 us (0.74)
  local copies, waits for them, and re-layouts: 70.2 us -> 16.3 us
  matrix products: 20 us -> 0 us
  Pallas kernels: 170 us -> 184 us
  other arithmetic: 10.1 us -> 1.73 us
    unnamed x141 -> x18, local copies, waits for them, and re-layouts: 37.2 us -> 9.74 us
    pallas_call x4 -> x2, Pallas kernels: 101 us -> 123 us  [the longest x1 81.7 us: back(): pl.pallas_call(back_kernel, name='back', out_shape=(jax.ShapeDtypeStruct(...]
    dot_general x16 -> x0, matrix products: 20 us -> none  [the longest x1 3.5 us: local(): jnp.einsum('rd,rf->df', act_two, d_gate_b, preferred_element_type=f32)]
    another operation x5 -> x8, local copies, waits for them, and re-layouts: 18.2 us -> 2.82 us  [local(): jnp.stack([wide(g) for g in (gain_in, gain_query, gain_key, gain_post_att...]
    reshape x17 -> x0, local copies, waits for them, and re-layouts: 7.69 us -> none  [the longest x6 3.07 us: local(): g.reshape(128, -1)]
    pallas_call x1, Pallas kernels: 69.2 us -> 61.9 us  [front(): pl.pallas_call(front_kernel, name='front', out_shape=(full(320, 1024), fu...]
where the time goes in v2:
time: 204 us
  Pallas kernels  184 us (90%)
  local copies, waits for them, and re-layouts  16.3 us (8%)
    pallas_call x1, Pallas kernels, back(): pl.pallas_call(back_kernel, name='back', out_shape=(jax.ShapeDtypeStruct(...  81.7 us
    pallas_call x1, Pallas kernels, front(): pl.pallas_call(front_kernel, name='front', out_shape=(full(320, 1024), fu...  61.9 us
    pallas_call x1, Pallas kernels, middle(): pl.pallas_call(middle_kernel, name='middle', out_shape=(jax.ShapeDtypeStr...  40.8 us
    unnamed x18, local copies, waits for them, and re-layouts  9.74 us

profile of v2, /device:TPU:0, one launch (start us, length us, event | category | flops | bytes accessed | tf_op | source)
XLA Modules:
  0.0 203.9 jit_solution(7948579556750972137)
XLA Ops:
  0.6 1.2 dynamic_slice.3.pair
  2.5 0.7 fusion.2
  3.2 0.8 select_reduce_fusion.inverse
  4.0 0.7 stack.24
  4.7 0.7 stack.27
  5.4 0.7 stack.28
  6.1 0.7 stack.29
  6.7 0.7 pad.7
  7.4 0.7 pad.8
  8.2 0.3 multiply_sine_fusion
  8.5 0.0 copy-start.2
  8.5 0.9 copy-done.2
  9.4 0.0 copy-start.3
  9.4 0.0 copy-start.4
  9.4 61.9 %front.1 = (bf16[2,320,1024]{2,1,0:T(8,128)(2,1)S(1)}, bf16[2,320,512]{2,1,0:T(8,128)(2,1)S(1)}, bf16[2,512,640]{2,1,0:T(8,128)(2,1)S(1)}, bf16[2,320,2048]{2,1,...) custom-call(bf16[320,1024]{1,0:T(8,128)(2,1)} %wq.1, ...), custom_call_target="tpu_custom_call" | custom-call | tf_op jit(solution)/shard_map/front/pallas_call | solution.py:373
  71.4 0.0 copy-start.1
  71.4 1.9 copy-done.1
  73.3 0.0 copy-done.3
  73.3 0.0 copy-done.4
  73.3 40.8 %middle.1 = (bf16[128,640]{1,0:T(8,128)(2,1)}, f32[128,640]{1,0:T(8,128)S(1)}, f32[512,256]{1,0:T(8,128)S(1)}, bf16[64,128,256]{2,1,0:T(8,128)(2,1)S(1)}, bf16[6...) custom-call(s32[64]{0:T(128)S(1)} %select_reduce_fusion.inverse, ...), custom_call_target="tpu_custom_call" | custom-call | tf_op jit(solution)/shard_map/middle/pallas_call | solution.py:926
  114.1 0.0 copy-start
  114.1 1.9 copy-done
  116.0 81.7 %back.1 = (bf16[128,640]{1,0:T(8,128)(2,1)S(1)}, f32[5,1024]{1,0:T(8,128)S(1)}, f32[5,256]{1,0:T(8,128)S(1)}, f32[5,256]{1,0:T(8,128)S(1)}, f32[8,640]{1,0:T(8,1...) custom-call(bf16[2,4,4,2,128,256]{5,4,3,2,1,0:T(8,128)(2,1)S(1)} %bitcast, ...), custom_call_target="tpu_custom_call" | custom-call | tf_op jit(solution)/shard_map/back/pallas_call | solution.py:1120
  197.8 0.6 slice_bitcast_fusion.3
  198.3 0.6 slice_bitcast_fusion
  198.9 0.7 copy.39
  199.6 0.6 copy.40
  200.2 0.6 copy.41
  200.8 0.6 copy.42
  201.4 0.6 copy.43
  202.0 0.6 copy.44
  202.7 0.6 copy.45
  203.3 0.6 copy.46
  (5 shorter events, 0.1 us)
Async XLA Ops:
  8.5 0.9 copy-start.2
  9.4 63.9 %copy-start.3 = (bf16[1,128,640]{2,1,0:T(8,128)(2,1)S(1)}, bf16[1,128,640]{2,1,0:T(8,128)(2,1)}, u32[]{:S(2)}) copy-start(bf16[1,128,640]{2,1,0:T(8,128)(2,1)} %param.16) | copy-start | bytes 491524
  9.4 63.9 %copy-start.4 = (bf16[1,128,640]{2,1,0:T(8,128)(2,1)S(1)}, bf16[1,128,640]{2,1,0:T(8,128)(2,1)}, u32[]{:S(2)}) copy-start(bf16[1,128,640]{2,1,0:T(8,128)(2,1)} %param.31) | copy-start | bytes 491524
  71.4 1.9 copy-start.1
  114.1 1.9 copy-start

commit v3 on v2

--- a/solution.py
+++ b/solution.py
@@ -124,6 +124,11 @@
     return ring
 
 
+def gain_row(gains, name):
+    first, n = {"in": (0, 5), "post_attn": (5, 5), "pre_ff": (10, 5), "post_ff": (15, 5), "query": (20, 2), "key": (22, 2)}[name]
+    return jnp.concatenate([gains[i : i + 1, :] for i in range(first, first + n)], axis=1)
+
+
 class PairGather:
     def __init__(self, links, axis, me, axis2, me2, piece, swap):
         self.links, self.axis, self.me, self.axis2, self.me2 = links, axis, me, axis2, me2
@@ -181,21 +186,22 @@
     o = 1 - h
     cross = device(1 - h, 1 - xl, z, y, core)
     other = device(h, 1 - xl, z, y, core)
-    locals_ = []
-    for i, (src, dst) in enumerate(
-        (
-            (wq, oq.at[h]),
-            (wk, okv.at[h, :, pl.ds(0, 256)]),
-            (wv, okv.at[h, :, pl.ds(256, 256)]),
-            (wg, og.at[h]),
-            (wu, ou.at[h]),
-            (wd, od.at[h]),
-            (wo, oo.at[h]),
+    locals_ = [
+        pltpu.make_async_copy(src, dst, local_sems.at[i])
+        for i, (src, dst) in enumerate(
+            (
+                (wk, okv.at[h, :, pl.ds(0, 256)]),
+                (wv, okv.at[h, :, pl.ds(256, 256)]),
+                (wq, oq.at[h]),
+                (wo, oo.at[h]),
+                (wg, og.at[h]),
+                (wd, od.at[h]),
+                (wu, ou.at[h]),
+            )
         )
-    ):
-        copy = pltpu.make_async_copy(src, dst, local_sems.at[i])
+    ]
+    for copy in locals_[:3]:
         copy.start()
-        locals_.append(copy)
     greet(
         [cross, other, sibling()]
         + [axis_neighbour(a, s) for a in ("y", "z") for s in (1, 3)]
@@ -211,71 +217,78 @@
     def piece_g(ref, yy, zz):
         return ref.at[rows(yy, 80), cols(core * 1024 + zz * 256, 256)]
 
-    def piece_kv(ref, yy, zz):
-        return ref.at[rows(yy, 80), cols(zz * 128, 128)]
-
     def piece_o(ref, yy, zz):
-        return ref.at[rows((core * 4 + zz) * 4 + yy, 16)]
-
-    for copy in locals_[:3]:
-        copy.wait()
-    crosses = [links.send(piece_kv(okv.at[h], y, z), piece_kv(okv.at[h], y, z), cross)]
-    for copy in locals_[3:]:
-        copy.wait()
-    crosses += [
-        links.send(piece(dst.at[h], y, z), piece(dst.at[h], y, z), cross)
-        for dst, piece in ((og, piece_g), (oo, piece_o), (ou, piece_g))
-    ]
+        return ref.at[rows((core * 4 + yy) * 4 + zz, 16)]
+
     half_q = lambda ref: ref.at[:, cols(core * 512, 512)]
     half_d = lambda ref: ref.at[rows(core, 512)]
+    half_u = lambda ref: ref.at[:, cols(core * 1024, 1024)]
+    half_kv = lambda ref: ref.at[:, cols(core * 256, 256)]
+    for copy in locals_[:2]:
+        copy.wait()
+    direct_kv = links.send(half_kv(okv.at[h]), half_kv(okv.at[h]), cross)
+    crosses = [
+        links.send(piece_g(wg, y, z), piece_g(og.at[h], y, z), cross),
+        links.send(piece_o(wo, y, z), piece_o(oo.at[h], y, z), cross),
+    ]
+    locals_[2].wait()
     direct_q = links.send(half_q(oq.at[h]), half_q(oq.at[h]), cross)
+    for copy in locals_[3:]:
+        copy.start()
     g, u, q, d, w, kv = og.at[o], ou.at[o], oq.at[o], od.at[o], oo.at[o], okv.at[o]
     swaps = []
 
     def swap(piece):
         swaps.append(links.send(piece, piece, sibling()))
 
+    states = inputs[...].astype(F32)
+    act = norm_scale(states, gain_row(gains, "in")).astype(BF16)
+    act_out[...] = act
+    direct_kv.wait_recv()
+    swap_kv = links.send(half_kv(kv), half_kv(kv), sibling())
     crosses[0].wait_recv()
-    kv1 = ring_of(
-        links, "z", z,
-        (
-            lambda i: piece_kv(kv, y, i),
-            lambda i, k: kv.at[
-                pl.ds(pl.multiple_of(y * 80 + k * 48, 16), 32 if k else 48), cols(i * 128, 128)
-            ],
-        ),
-    )
-    for copy in crosses[1:3]:
-        copy.wait_recv()
     a1 = ring_of(
         links, "y", y,
         (
             lambda i: piece_g(g, i, z),
             lambda i, k: g.at[rows(i, 80), cols(core * 1024 + z * 256 + k * 128, 128)],
         ),
-        (
-            lambda i: piece_o(w, i, z),
-            lambda i, k: w.at[
-                rows((core * 4 + z) * 4 + i, 16), pl.ds(384 * k, 256 if k else 384)
-            ],
-        ),
-    )
-    crosses[3].wait_recv()
+    )
+    crosses[1].wait_recv()
     b1 = ring_of(
         links, "z", z,
         (
-            lambda i: piece_g(u, y, i),
-            lambda i, k: u.at[rows(y, 80), cols(core * 1024 + i * 256 + k * 128, 128)],
+            lambda i: piece_o(w, y, i),
+            lambda i, k: w.at[
+                rows((core * 4 + y) * 4 + i, 16), pl.ds(384 * k, 256 if k else 384)
+            ],
         ),
     )
-    kv1.relay()
+    swap_kv.wait_recv()
+
+    kv_lin = jnp.dot(act, okv[...].reshape(640, 512), preferred_element_type=F32)
+    key_lin_out[...] = kv_lin[:, :256]
+    cos, sin = cosine[...], sine[...]
+
+    def turned(lin, gain):
+        n = norm_scale(lin, gain)
+        a, b = n[:, :128], n[:, 128:]
+        return jnp.concatenate([a * cos - b * sin, b * cos + a * sin], axis=1).astype(BF16)
+
+    k_all[xl, z, y, core] = turned(kv_lin[:, :256], gain_row(gains, "key"))
+    v_all[xl, z, y, core] = kv_lin[:, 256:].astype(BF16)
+    own = lambda ref: ref.at[xl, z, y, core]
+    first = [links.send(own(ref), own(ref), other) for ref in (k_all, v_all)]
+    keys = PairGather(links, "y", y, "z", z, lambda p, i, j: k_all.at[p, j, i, core], swap)
+    values = PairGather(links, "z", z, "y", y, lambda p, i, j: v_all.at[p, i, j, core], swap)
+    keys.begin(xl)
+    values.begin(xl)
+    locals_[5].wait()
+    direct_d = links.send(half_d(od.at[h]), half_d(od.at[h]), cross)
+    locals_[6].wait()
+    direct_u = links.send(half_u(ou.at[h]), half_u(ou.at[h]), cross)
     a1.relay()
     b1.relay()
-    kv1.finish()
-    kv2 = ring_of(
-        links, "y", y,
-        (lambda i: kv.at[rows(i, 80)], lambda i, k: kv.at[rows(i, 80), pl.ds(256 * k, 256)]),
-    )
     a1.finish()
     a2 = ring_of(
         links, "z", z,
@@ -283,51 +296,26 @@
             lambda i: g.at[:, cols(core * 1024 + i * 256, 256)],
             lambda i, k: g.at[pl.ds(160 * k, 160), cols(core * 1024 + i * 256, 256)],
         ),
+    )
+    b1.finish()
+    b2 = ring_of(
+        links, "y", y,
         (
             lambda i: w.at[rows(core * 4 + i, 64)],
             lambda i, k: w.at[rows((core * 4 + i) * 2 + k, 32)],
         ),
     )
-    b1.finish()
-    kv2.relay()
-    b2 = ring_of(
-        links, "y", y,
-        (
-            lambda i: u.at[rows(i, 80), cols(core * 1024, 1024)],
-            lambda i, k: u.at[rows(i, 80), cols(core * 1024 + k * 512, 512)],
-        ),
-    )
-    kv2.finish()
-
-    states = inputs[...].astype(F32)
-    act = norm_scale(states, gains[0:1]).astype(BF16)
-    act_out[...] = act
-    kv_lin = jnp.dot(act, okv[...].reshape(640, 512), preferred_element_type=F32)
-    key_lin_out[...] = kv_lin[:, :256]
-    cos, sin = cosine[...], sine[...]
-
-    def turned(lin, gain):
-        n = norm_scale(lin, gain)
-        a, b = n[:, :128], n[:, 128:]
-        return jnp.concatenate([a * cos - b * sin, b * cos + a * sin], axis=1).astype(BF16)
-
-    k_all[xl, z, y, core] = turned(kv_lin[:, :256], gains[2:3, :256])
-    v_all[xl, z, y, core] = kv_lin[:, 256:].astype(BF16)
-    own = lambda ref: ref.at[xl, z, y, core]
-    first = [links.send(own(ref), own(ref), other) for ref in (k_all, v_all)]
-    keys = PairGather(links, "y", y, "z", z, lambda p, i, j: k_all.at[p, j, i, core], swap)
-    values = PairGather(links, "z", z, "y", y, lambda p, i, j: v_all.at[p, i, j, core], swap)
-    keys.begin(xl)
-    values.begin(xl)
-    direct_q.wait_recv()
-    swap(half_q(q))
-    swap_q = swaps.pop()
-    direct_d = links.send(half_d(od.at[h]), half_d(od.at[h]), cross)
-    a2.relay()
-    b2.relay()
     for copy, gather in zip(first, (keys, values)):
         copy.wait_recv()
         gather.begin(1 - xl)
+    for gather in (keys, values):
+        gather.middle(xl)
+    for gather in (keys, values):
+        gather.middle(1 - xl)
+    direct_q.wait_recv()
+    swap_q = links.send(half_q(q), half_q(q), sibling())
+    a2.relay()
+    b2.relay()
     swap_q.wait_recv()
     for head in range(4):
         lin = jnp.dot(
@@ -336,32 +324,30 @@
             preferred_element_type=F32,
         )
         query_lin_out[:, head * 256 : (head + 1) * 256] = lin
-        row = turned(lin, gains[1:2, :256])
+        row = turned(lin, gain_row(gains, "query"))
         query_out[head * 64 : (head + 1) * 64] = row[:64]
         query_out[256 + head * 64 : 256 + (head + 1) * 64] = row[64:]
 
-    for gather in (keys, values):
-        gather.middle(xl)
-    for gather in (keys, values):
-        gather.middle(1 - xl)
     a2.finish()
     b2.finish()
     swap(g.at[:, cols(core * 1024, 1024)])
-    swap(u.at[:, cols(core * 1024, 1024)])
     swap(w.at[rows(core, 256)])
-    direct_d.wait_recv()
-    swap(half_d(d))
     for k in range(8):
         for gather in (keys, values):
             gather.relay(k)
+    for direct, half, ref in ((direct_d, half_d, d), (direct_u, half_u, u)):
+        direct.wait_recv()
+        swap(half(ref))
     for k in range(8):
         for gather in (keys, values):
             gather.finish(k)
-    for ring in (kv1, kv2, a1, b1, a2, b2, keys, values):
+    for ring in (a1, b1, a2, b2, keys, values):
         ring.drain()
-    for copy in crosses + [direct_q, direct_d, swap_q] + first:
+    for copy in crosses + [direct_kv, direct_q, direct_d, direct_u, swap_kv, swap_q] + first:
         copy.wait_send()
     for copy in swaps:
+        copy.wait()
+    for copy in locals_[3:5]:
         copy.wait()
 
 
@@ -369,7 +355,7 @@
     wq, wk, wv, wo, wg, wu, wd = weights
     full = lambda rows, width: pltpu.VMEM((2, rows, width), BF16)
     kv = pltpu.VMEM((2, 4, 4, 2, 128, 256), BF16)
-    count = 4 + 2 + 2 + 4 * (2 + 4 + 2) + 2 * (2 + 8) * 4 + 2 * 8 * 4 + 5
+    count = 2 + 4 + 2 + 4 + 2 + 4 * 4 + 2 * (2 + 8) * 4 + 2 * 8 * 4
     outs = pl.pallas_call(
         front_kernel,
         name="front",
@@ -808,26 +794,18 @@
     return dot(act, chosen).astype(BF16)
 
 
-def spread_rows(flat, act, grad, rows, first=0):
+def spread_rows(flat, act, grad, rows, first=0, count=128):
     tiles = grad.shape[1] // 128
     for t in range(5):
-        part = dot_tn(act[:, t * 128 : (t + 1) * 128], grad)
+        part = dot_tn(act[:, t * 128 + first : t * 128 + first + count], grad)
         for c in range(tiles):
-            flat[pl.ds(first + t * tiles + c, 128, stride=rows), :] = part[
-                :, c * 128 : (c + 1) * 128
-            ]
-
-
-def pack(out, flat, rows):
-    @pl.loop(0, 128)
-    def _(i):
-        out[i] = flat[pl.ds(pl.multiple_of(i * rows, 8), rows), :].astype(BF16)
+            flat[pl.ds(t * tiles + c, count, stride=rows), :] = part[:, c * 128 : (c + 1) * 128]
 
 
 def middle_kernel(
     inverse, pair, query, keys, values, inputs, cotangent, wo, wg, wu, wd, gains,
-    layer_out, grad_resid_out, d_query, d_keys, d_values, gr_down, gr_gate, gr_up, gr_out, gr_gains,
-    acc, weight, gate, upper, hidden, d_gate, d_upper, att, d_att_rows, flat,
+    layer_out, grad_resid_out, d_query, d_keys, d_values, act_two_out, hidden, d_down_out, d_gate, d_upper, att,
+    d_att_out, gr_gains, acc, weight, gate, upper, d_att_rows,
 ):
     own = pair[0]
     attend(own, inverse, query, keys, values, acc, weight)
@@ -846,19 +824,21 @@
             ]
 
     att_lin = dot(att[...], wo[...])
-    resid = inputs[...].astype(F32) + norm_scale(att_lin, gains[3:4])
-    act_two = norm_scale(resid, gains[4:5]).astype(BF16)
+    resid = inputs[...].astype(F32) + norm_scale(att_lin, gain_row(gains, "post_attn"))
+    act_two = norm_scale(resid, gain_row(gains, "pre_ff")).astype(BF16)
+    act_two_out[...] = act_two
     for c in range(4):
         s = slice(c * 512, (c + 1) * 512)
         gate[:, s] = dot(act_two, wg[:, s])
         upper[:, s] = dot(act_two, wu[:, s])
         hidden[:, s] = (gelu_terms(gate[:, s])[0] * upper[:, s]).astype(BF16)
     down = dot(hidden[...], wd[...])
-    layer_out[...] = (resid + norm_scale(down, gains[5:6])).astype(BF16)
+    layer_out[...] = (resid + norm_scale(down, gain_row(gains, "post_ff"))).astype(BF16)
 
     grad_y = cotangent[...].astype(F32)
-    d_down, d_post_ff = norm_back(down, gains[5:6], grad_y)
+    d_down, d_post_ff = norm_back(down, gain_row(gains, "post_ff"), grad_y)
     d_down = d_down.astype(BF16)
+    d_down_out[...] = d_down
     d_act_two = jnp.zeros((128, 640), F32)
     for c in range(4):
         s = slice(c * 512, (c + 1) * 512)
@@ -869,11 +849,12 @@
         d_gate[:, s] = a
         d_upper[:, s] = b
         d_act_two = d_act_two + dot_nt(a, wg[:, s]) + dot_nt(b, wu[:, s])
-    d_resid, d_pre_ff = norm_back(resid, gains[4:5], d_act_two)
+    d_resid, d_pre_ff = norm_back(resid, gain_row(gains, "pre_ff"), d_act_two)
     grad_resid = grad_y + d_resid
     grad_resid_out[...] = grad_resid
-    d_att, d_post_attn = norm_back(att_lin, gains[3:4], grad_resid)
+    d_att, d_post_attn = norm_back(att_lin, gain_row(gains, "post_attn"), grad_resid)
     d_att = d_att.astype(BF16)
+    d_att_out[...] = d_att
     gr_gains[...] = jnp.concatenate(
         [d_post_attn, d_pre_ff, d_post_ff, jnp.zeros((5, 640), F32)], axis=0
     )
@@ -891,82 +872,142 @@
         preferred_element_type=F32,
     )[:1]
 
-    @pl.loop(0, 16)
-    def _(i):
-        part = dot_tn(hidden[:, pl.ds(pl.multiple_of(i * 128, 128), 128)], d_down).astype(BF16)
-        for j in range(8):
-            for c in range(5):
-                gr_down[i * 8 + j, c * 16 : (c + 1) * 16, :] = part[
-                    j * 16 : (j + 1) * 16, c * 128 : (c + 1) * 128
-                ]
-
-    @pl.loop(0, 8)
-    def _(i):
-        part = dot_tn(att[:, pl.ds(pl.multiple_of(i * 128, 128), 128)], d_att)
-        for j in range(16):
-            rows = part[j * 8 : (j + 1) * 8]
-            gr_out[i * 16 + j] = jnp.concatenate(
-                [rows[:, c * 128 : (c + 1) * 128] for c in range(5)], axis=0
-            ).astype(BF16)
-
-    fives = by_fives(act_two)
-    spread_rows(flat, fives, d_gate[...], 80)
-    pack(gr_gate, flat, 80)
-    spread_rows(flat, fives, d_upper[...], 80)
-    pack(gr_up, flat, 80)
-
     attend_back(
         own, inverse, query, d_att_rows, log_sum, delta, keys, values, d_query, d_keys, d_values
     )
 
 
 def middle(*args):
-    block = lambda rows: pltpu.VMEM((128, rows, 128), BF16)
     kv = pltpu.VMEM((64, 128, 256), BF16)
+    act = lambda width: jax.ShapeDtypeStruct((128, width), BF16)
     return pl.pallas_call(
         middle_kernel,
         name="middle",
         out_shape=(
-            jax.ShapeDtypeStruct((128, 640), BF16),
+            act(640),
             jax.ShapeDtypeStruct((128, 640), F32),
             jax.ShapeDtypeStruct((512, 256), F32),
-            kv, kv, block(80), block(80), block(80), block(40),
+            kv, kv, act(640), act(2048), act(640), act(2048), act(2048), act(1024), act(640),
             jax.ShapeDtypeStruct((8, 640), F32),
         ),
         in_specs=[SMEM, SMEM] + [VMEM] * 10,
-        out_specs=(VMEM,) * 10,
+        out_specs=(VMEM,) * 13,
         scratch_shapes=[
             pltpu.VMEM((512, 256), F32),
             pltpu.VMEM((512, 128), F32),
             pltpu.VMEM((128, 2048), F32),
             pltpu.VMEM((128, 2048), F32),
-            pltpu.VMEM((128, 2048), BF16),
-            pltpu.VMEM((128, 2048), BF16),
-            pltpu.VMEM((128, 2048), BF16),
-            pltpu.VMEM((128, 1024), BF16),
             pltpu.VMEM((512, 256), BF16),
-            pltpu.VMEM((128 * 80, 128), F32),
         ],
-        compiler_params=pltpu.CompilerParams(vmem_limit_bytes=23 << 20),
+        compiler_params=pltpu.CompilerParams(vmem_limit_bytes=16 << 20),
     )(*args)
 
 
-FIRST_ROWS, FIRST_ORDERS = (80, 80, 80, 40), ("xyz", "xzy", "yzx", "zxy")
-LAST_ROWS, LAST_ORDERS = (40, 32), ("xyz", "yzx")
-
-
-def pack_places(out, flat, rows):
-    @pl.loop(0, 128)
+FIRST_ROWS, FIRST_ORDERS = (80, 40, 80, 80, 40), ("xyz", "zxy", "xzy", "yzx", "xyz")
+LAST_ROWS, LAST_ORDERS = (16, 16), ("yzx", "zxy")
+
+
+def spot(i):
+    return (i // 64, (i // 16) % 4, (i // 4) % 4, (i // 2) % 2, i % 2)
+
+
+def pack_places(out, flat, rows, first=0, size=None, start=0, count=128):
+    @pl.loop(0, count // 4)
+    def _(block):
+        for j in range(4):
+            i = block * 4 + j
+            out[spot(start + i)] = flat[
+                pl.ds(pl.multiple_of(i * rows + first, 8), size or rows), :
+            ].astype(BF16)
+
+
+def cut_by_fives(out, flat, act, grad):
+    for start in (0, 64):
+        spread_rows(flat, act, grad, 80, start, 64)
+        pack_places(out, flat, 80, start=start, count=64)
+
+
+def by_sixteens(out, act, grad):
+    @pl.loop(0, 16)
     def _(i):
-        out[i // 64, (i // 16) % 4, (i // 4) % 4, (i // 2) % 2, i % 2] = flat[
-            pl.ds(pl.multiple_of(i * rows, 8), rows), :
-        ].astype(BF16)
+        part = dot_tn(act[:, pl.ds(pl.multiple_of(i * 128, 128), 128)], grad).astype(BF16)
+        for j in range(8):
+            for c in range(5):
+                out[spot(i * 8 + j) + (pl.ds(c * 16, 16),)] = part[
+                    j * 16 : (j + 1) * 16, c * 128 : (c + 1) * 128
+                ]
+
+
+def by_eights(out, act, grad):
+    @pl.loop(0, 8)
+    def _(i):
+        part = dot_tn(act[:, pl.ds(pl.multiple_of(i * 128, 128), 128)], grad)
+        for j in range(16):
+            rows = part[j * 8 : (j + 1) * 8]
+            out[spot(i * 16 + j)] = jnp.concatenate(
+                [rows[:, c * 128 : (c + 1) * 128] for c in range(5)], axis=0
+            ).astype(BF16)
+
+
+class DirectSum:
+    SCRATCH = 6
+    DIMS = WeightSum.DIMS
+
+    def __init__(self, links, source, out, scratch, axes):
+        h, xl, z, y, core = place()
+        self.links, self.source, self.out, self.axes = links, source, out, axes
+        self.core, self.me = core, {"x": 2 * h + xl, "y": y, "z": z}
+        self.total, self.last = scratch[:3], scratch[3:]
+        self.dims = [self.DIMS]
+        for axis in axes:
+            self.dims.append(without(self.dims[-1], axis))
+
+    @classmethod
+    def scratch(cls, rows, axes):
+        buf = lambda *lead: pltpu.VMEM(lead + (rows, 128), BF16)
+        two = without(cls.DIMS, axes[0])
+        three = without(two, axes[1])
+        a, b = sizes(two), sizes(three)
+        return [buf(*sizes(cls.DIMS)), buf(*a), buf(*b), buf(3, *a), buf(3, *b), buf(3)]
+
+    def swap(self):
+        self.copy = self.links.send(
+            self.source.at[:, :, :, 1 - self.core], self.total[0], sibling()
+        )
+
+    def start(self):
+        self.copy.wait_recv()
+        add_into(self.total[0], self.source.at[:, :, :, self.core])
+        self.stages = []
+        self.send()
+
+    def send(self):
+        n = len(self.stages)
+        axis = self.axes[n]
+        stage = Direct(
+            self.links, axis, self.me[axis],
+            lambda i: pick(self.total[n], self.dims[n], axis, i)[0], self.last[n],
+        )
+        stage.start()
+        self.stages.append(stage)
+
+    def next(self):
+        self.stages[-1].finish(self.total[len(self.stages)])
+        self.send()
+
+    def finish(self):
+        self.stages[-1].finish(self.out)
+
+    def drain(self):
+        for stage in self.stages:
+            stage.drain()
+        self.copy.wait_send()
 
 
 def project_back(
     d_query, d_key, d_value, query_lin, key_lin, act_one, inputs, wq, wkv, gains, cosine, sine, grad_resid, d_gains,
     input_grad, gr_query, gr_tail,
-    d_query_lin, d_kv_lin, flat, flat_tail,
+    d_query_lin, d_kv_lin, flat,
 ):
     cos, sin = cosine[...], sine[...]
 
@@ -982,21 +1023,22 @@
         grad = jnp.concatenate(
             [d_query[b * 256 + head * 64 : b * 256 + (head + 1) * 64] for b in range(2)], axis=0
         )
-        d_lin, d_gain = turn_back(query_lin[:, cut], gains[1:2, :256], grad)
+        d_lin, d_gain = turn_back(query_lin[:, cut], gain_row(gains, "query"), grad)
         d_query_lin[:, cut] = d_lin.astype(BF16)
         d_gain_query = d_gain_query + d_gain
     spread_rows(flat, fives, d_query_lin[...], 40)
     pack_places(gr_query, flat, 40)
     d_act = dot_nt(d_query_lin[...], wq[...])
     yield
-    d_lin, d_gain_key = turn_back(key_lin[...], gains[2:3, :256], d_key[...])
+    d_lin, d_gain_key = turn_back(key_lin[...], gain_row(gains, "key"), d_key[...])
     d_kv_lin[:, :256] = d_lin.astype(BF16)
     d_kv_lin[:, 256:] = d_value[...].astype(BF16)
     d_act = d_act + dot_nt(d_kv_lin[...], wkv[...])
-    d_states, d_gain_in = norm_back(inputs[...].astype(F32), gains[0:1], d_act)
+    d_states, d_gain_in = norm_back(inputs[...].astype(F32), gain_row(gains, "in"), d_act)
     input_grad[...] = (grad_resid[...] + d_states).astype(BF16)
-    flat_tail[...] = jnp.zeros_like(flat_tail)
-    spread_rows(flat_tail, fives, d_kv_lin[...], 32)
+    for row in range(21, 32):
+        flat[pl.ds(row, 128, stride=32), :] = jnp.zeros((128, 128), F32)
+    spread_rows(flat, fives, d_kv_lin[...], 32)
     total = jnp.zeros((128, 128), F32)
     column = 0
     for row, each in (
@@ -1010,14 +1052,15 @@
         n = 128 * each
         owner = lax.broadcasted_iota(jnp.int32, (128, n), 1) // each
         mine = owner == lax.broadcasted_iota(jnp.int32, (128, n), 0)
-        spot = lax.broadcasted_iota(jnp.int32, (n, 128), 0) % each + column
-        here = spot == lax.broadcasted_iota(jnp.int32, (n, 128), 1)
+        where = lax.broadcasted_iota(jnp.int32, (n, 128), 0) % each + column
+        here = where == lax.broadcasted_iota(jnp.int32, (n, 128), 1)
         total = total + dot(
             jnp.where(mine, row, 0.0).astype(BF16), here.astype(F32).astype(BF16)
         )
         column += each
-    flat_tail[pl.ds(20, 128, stride=32), :] = total
-    pack_places(gr_tail, flat_tail, 32)
+    flat[pl.ds(20, 128, stride=32), :] = total
+    for k in range(2):
+        pack_places(gr_tail[k], flat, 32, 16 * k, 16)
     yield
 
 
@@ -1029,13 +1072,15 @@
         del refs[:n]
         return some
 
-    kv_sources, first_sources, others = take(2), take(4), take(12)
+    kv_sources, acts, others = take(2), take(7), take(12)
     input_grad, o_query, o_key, o_value, o_output, o_gate, o_up, o_down, o_gains = take(9)
     kv_sums = take(2)
-    first_sums, last_sources, last_sums, temps = take(4), take(2), take(2), take(4)
+    first_sums, last_sums = take(5), take(2)
+    first_sources, last_sources = take(5), take(2)
+    d_query_lin, d_kv_lin, flat = take(3)
     kv_scratch = [take(KeySum.SCRATCH) for _ in range(2)]
-    first_scratch = [take(WeightSum.SCRATCH) for _ in range(4)]
-    last_scratch = [take(WeightSum.SCRATCH) for _ in range(2)]
+    first_scratch = [take(WeightSum.SCRATCH) for _ in range(5)]
+    last_scratch = [take(DirectSum.SCRATCH) for _ in range(2)]
     send_sems, recv_sems = refs
     greet(
         [sibling()] + [axis_neighbour(a, s) for a in ("x", "y", "z") for s in (1, 2, 3)]
@@ -1050,72 +1095,97 @@
         for args in zip(first_sources, first_sums, first_scratch, FIRST_ORDERS)
     ]
     final = [
-        WeightSum(links, *args)
+        DirectSum(links, *args)
         for args in zip(last_sources, last_sums, last_scratch, LAST_ORDERS)
     ]
+    down, output, gate, up, query = first
+    act_two, hidden, d_down, d_gate, d_upper, att, d_att = acts
+    projections = project_back(
+        others[0], *kv_sums, *others[1:], input_grad, first_sources[4], last_sources,
+        d_query_lin, d_kv_lin, flat,
+    )
 
     def run(group, *stages):
         for stage in stages:
             for s in group:
                 getattr(s, stage)()
 
-    d_query, query_lin = others[:2]
-    projections = project_back(
-        d_query, *kv_sums, *others[1:], input_grad, *last_sources, *temps
-    )
-    run(kv, "swap")
-    run(first, "swap")
-    run(kv, "start")
-    run(first, "start")
+    run(kv, "swap", "start")
+    by_sixteens(first_sources[0], hidden, d_down[...])
+    down.swap()
+    run(kv, "relay")
+    by_eights(first_sources[1], att, d_att[...])
+    output.swap()
+    down.start()
+    output.start()
+    fives = by_fives(act_two[...])
+    cut_by_fives(first_sources[2], flat, fives, d_gate[...])
+    gate.swap()
+    run(kv, "next")
+    down.relay()
+    output.relay()
+    gate.start()
+    run(kv, "relay2")
+    cut_by_fives(first_sources[3], flat, fives, d_upper[...])
+    up.swap()
+    run(kv, "next2")
+    up.start()
+    down.next()
+    output.next()
     next(projections)
-    run(kv, "relay")
-    run(first, "relay")
-    run(kv, "next", "relay2", "next2")
-    run(first, "next")
+    query.swap()
     run(kv, "finish")
     next(projections)
-    run(final, "swap", "start")
-    run(first, "relay2", "next2")
-    run(final, "relay", "next", "relay2", "next2")
+    run(final, "swap")
+    query.start()
+    run(final, "start")
+    gate.relay()
+    up.relay()
+    query.relay()
+    run(final, "next")
+    run([down, output], "relay2")
+    run([gate, up, query], "next")
+    run(final, "next")
+    run([down, output], "next2")
+    run([gate, up, query], "relay2", "next2")
+    run(final, "finish")
     run(first, "finish")
-    run(final, "finish")
     run(kv + first + final, "drain")
 
-    s_down, s_gate, s_up, s_output = first_sums
-    s_query, s_tail = last_sums
+    s_down, s_output, s_gate, s_up, s_query = first_sums
+    s_tail = jnp.concatenate([part[...] for part in last_sums], axis=0)
     for c in range(5):
         cut = slice(c * 128, (c + 1) * 128)
         o_down[:, cut] = s_down[c * 16 : (c + 1) * 16, :]
         o_output[:, cut] = s_output[c * 8 : (c + 1) * 8, :]
-    for out, source, first_row, step, tiles in (
-        (o_gate, s_gate, 0, 16, 16),
-        (o_up, s_up, 0, 16, 16),
-        (o_query, s_query, 0, 8, 8),
-        (o_key, s_tail, 0, 4, 2),
-        (o_value, s_tail, 2, 4, 2),
-    ):
-        for c in range(tiles):
-            out[:, c * 128 : (c + 1) * 128] = source[pl.ds(first_row + c, 5, stride=step), :]
-    o_gains[...] = s_tail[20:21, :]
-
-
-def back(kv, grads, others):
+    for out, source, step in ((o_gate, s_gate, 16), (o_up, s_up, 16), (o_query, s_query, 8)):
+        for c in range(step):
+            out[:, c * 128 : (c + 1) * 128] = source[pl.ds(c, 5, stride=step), :]
+    for t in range(5):
+        for c in range(2):
+            cut = slice(c * 128, (c + 1) * 128)
+            o_key[t : t + 1, cut] = s_tail[t * 4 + c : t * 4 + c + 1]
+            o_value[t : t + 1, cut] = s_tail[t * 4 + c + 2 : t * 4 + c + 3]
+    o_gains[...] = s_tail[20:21]
+
+
+def back(kv, acts, others):
     buf = lambda *shape: pltpu.VMEM(shape, F32)
     scratch = [buf(128, 256)] * 2
-    scratch += [buf(rows, 128) for rows in FIRST_ROWS]
-    scratch += [pltpu.VMEM((2, 4, 4, 2, 2, rows, 128), BF16) for rows in LAST_ROWS]
-    scratch += [buf(rows, 128) for rows in LAST_ROWS]
+    scratch += [buf(rows, 128) for rows in FIRST_ROWS + LAST_ROWS]
+    scratch += [pltpu.VMEM((2, 4, 4, 2, 2, rows, 128), BF16) for rows in FIRST_ROWS + LAST_ROWS]
     scratch += [
         pltpu.VMEM((128, 1024), BF16),
         pltpu.VMEM((128, 512), BF16),
-        buf(128 * 40, 128),
-        buf(128 * 32, 128),
+        buf(64 * 80, 128),
     ]
     for _ in kv:
         scratch += KeySum.scratch()
-    for rows, order in zip(FIRST_ROWS + LAST_ROWS, FIRST_ORDERS + LAST_ORDERS):
+    for rows, order in zip(FIRST_ROWS, FIRST_ORDERS):
         scratch += WeightSum.scratch(rows, order)
-    count = 2 * 17 + 6 * 19
+    for rows, order in zip(LAST_ROWS, LAST_ORDERS):
+        scratch += DirectSum.scratch(rows, order)
+    count = 2 * 17 + 5 * 19 + 2 * 10
     out = lambda rows, width: jax.ShapeDtypeStruct((rows, width), F32)
     return pl.pallas_call(
         back_kernel,
@@ -1125,16 +1195,16 @@
             out(5, 1024), out(5, 256), out(5, 256), out(8, 640), out(5, 2048), out(5, 2048),
             out(16, 640), out(1, 128),
         ),
-        in_specs=[VMEM] * 18,
+        in_specs=[VMEM] * 21,
         out_specs=(VMEM,) * 9,
         scratch_shapes=scratch
         + [pltpu.SemaphoreType.DMA((count,)), pltpu.SemaphoreType.DMA((count,))],
         compiler_params=pltpu.CompilerParams(
-            collective_id=2, has_side_effects=True, vmem_limit_bytes=36 << 20
+            collective_id=2, has_side_effects=True, vmem_limit_bytes=47 << 20
         ),
     )(
         *[g.reshape((2, 4, 4, 2) + g.shape[1:]) for g in kv],
-        *[g.reshape((2, 4, 4, 2, 2) + g.shape[1:]) for g in grads],
+        *acts,
         *others,
     )
 
@@ -1168,23 +1238,26 @@
     cosine, sine = jnp.cos(angles), jnp.sin(angles)
     matches = pair_order[None, :] == jnp.arange(64, dtype=jnp.int32)[:, None]
     inverse = jnp.sum(jnp.where(matches, jnp.arange(64, dtype=jnp.int32)[None, :], 0), axis=1)
-    wide = lambda g: jnp.pad(g, (0, 640 - g.shape[0]))
-    gains = jnp.stack(
-        [wide(g) for g in (gain_in, gain_query, gain_key, gain_post_attn, gain_pre_ff, gain_post_ff)]
-        + [jnp.zeros((640,), F32)] * 2
-    )
+    gains, first = jnp.zeros((3072,), F32), 0
+    for g in (gain_in, gain_post_attn, gain_pre_ff, gain_post_ff, gain_query, gain_key):
+        gains = gains + jnp.pad(g, (first, 3072 - first - g.shape[0]))
+        first += g.shape[0]
+    gains = gains.reshape(24, 128)
     (
         wq_all, wkv_all, wo_all, wg_all, wu_all, wd_all, keys, values,
         act_one, query_lin, key_lin, query,
     ) = front(
         (w_query, w_key, w_value, w_output, w_gate, w_up, w_down), inputs[0], gains, cosine, sine
     )
-    layer_out, grad_resid, d_query, d_keys, d_values, gr_down, gr_gate, gr_up, gr_out, d_gains = middle(
+    (
+        layer_out, grad_resid, d_query, d_keys, d_values, act_two, hidden, d_down, d_gate, d_upper, att, d_att,
+        d_gains,
+    ) = middle(
         inverse, own_pair, query, keys, values, inputs[0], cotangent[0],
         wo_all, wg_all, wu_all, wd_all, gains,
     )
     input_grad, s_query, s_key, s_value, s_output, s_gate, s_up, s_down, s_gains = back(
-        (d_keys, d_values), (gr_down, gr_gate, gr_up, gr_out),
+        (d_keys, d_values), (act_two, hidden, d_down, d_gate, d_upper, att, d_att),
         (d_query, query_lin, key_lin, act_one, inputs[0], wq_all, wkv_all, gains, cosine, sine, grad_resid, d_gains),
     )
     s_gains = s_gains[0]

time: 204 us -> 186 us (0.912)
  Pallas kernels: 184 us -> 170 us
  local copies, waits for them, and re-layouts: 16.3 us -> 12.2 us
    pallas_call x1, Pallas kernels: 40.8 us -> 27.9 us  [middle(): pl.pallas_call(middle_kernel, name='middle', out_shape=(act(640), jax.Sha...]
    another operation x8 -> x0, local copies, waits for them, and re-layouts: 2.82 us -> none  [local(): jnp.stack([wide(g) for g in (gain_in, gain_query, gain_key, gain_post_att...]
    pallas_call x1, Pallas kernels: 61.9 us -> 59.3 us  [front(): pl.pallas_call(front_kernel, name='front', out_shape=(full(320, 1024), fu...]
where the time goes in v3:
time: 186 us
  Pallas kernels  170 us (91%)
  local copies, waits for them, and re-layouts  12.2 us (7%)
  other arithmetic  2.52 us (1%)
    pallas_call x1, Pallas kernels, back(): pl.pallas_call(back_kernel, name='back', out_shape=(jax.ShapeDtypeStruct(...  82.7 us
    pallas_call x1, Pallas kernels, front(): pl.pallas_call(front_kernel, name='front', out_shape=(full(320, 1024), fu...  59.3 us
    pallas_call x1, Pallas kernels, middle(): pl.pallas_call(middle_kernel, name='middle', out_shape=(act(640), jax.Sha...  27.9 us
    unnamed x18, local copies, waits for them, and re-layouts  9.79 us

profile of v3, /device:TPU:0, one launch (start us, length us, event | category | flops | bytes accessed | tf_op | source)
XLA Modules:
  0.0 186.0 jit_solution(14499202534285597549)
XLA Ops:
  0.6 1.2 dynamic_slice.3.pair
  2.5 0.7 fusion.2
  3.2 0.8 select_reduce_fusion.inverse
  4.0 0.8 add_bitcast_fusion.gains.refs_16_
  4.8 0.3 multiply_sine_fusion
  5.1 0.0 copy-start.2
  5.1 0.9 copy-done.2
  6.0 0.0 copy-start.4
  6.0 59.3 %front.1 = (bf16[2,320,1024]{2,1,0:T(8,128)(2,1)S(1)}, bf16[2,320,512]{2,1,0:T(8,128)(2,1)S(1)}, bf16[2,512,640]{2,1,0:T(8,128)(2,1)S(1)}, bf16[2,320,2048]{2,1,...) custom-call(bf16[320,1024]{1,0:T(8,128)(2,1)} %wq.1, ...), custom_call_target="tpu_custom_call" | custom-call | tf_op jit(solution)/shard_map/front/pallas_call | solution.py:359
  65.3 0.0 copy-done.4
  65.3 0.0 copy-start.3
  65.3 27.9 %middle.1 = (bf16[128,640]{1,0:T(8,128)(2,1)}, f32[128,640]{1,0:T(8,128)S(1)}, f32[512,256]{1,0:T(8,128)S(1)}, bf16[64,128,256]{2,1,0:T(8,128)(2,1)S(1)}, bf16[6...) custom-call(s32[64]{0:T(128)S(1)} %select_reduce_fusion.inverse, ...), custom_call_target="tpu_custom_call" | custom-call | tf_op jit(solution)/shard_map/middle/pallas_call | solution.py:883
  93.2 0.0 copy-start
  93.2 1.9 %copy-done = bf16[64,128,256]{2,1,0:T(8,128)(2,1)} copy-done((bf16[64,128,256]{2,1,0:T(8,128)(2,1)}, bf16[64,128,256]{2,1,0:T(8,128)(2,1)S(1)}, u32[]{:S(2)}) %copy-start) | copy-done | bytes 4194328
  95.2 0.0 copy-start.1
  95.2 2.0 %copy-done.1 = bf16[64,128,256]{2,1,0:T(8,128)(2,1)} copy-done((bf16[64,128,256]{2,1,0:T(8,128)(2,1)}, bf16[64,128,256]{2,1,0:T(8,128)(2,1)S(1)}, u32[]{:S(2)}) %copy-start.1) | copy-done | bytes 4194328
  97.2 0.0 copy-done.3
  97.2 82.7 %back.1 = (bf16[128,640]{1,0:T(8,128)(2,1)S(1)}, f32[5,1024]{1,0:T(8,128)S(1)}, f32[5,256]{1,0:T(8,128)S(1)}, f32[5,256]{1,0:T(8,128)S(1)}, f32[8,640]{1,0:T(8,1...) custom-call(bf16[2,4,4,2,128,256]{5,4,3,2,1,0:T(8,128)(2,1)} %bitcast.30,, ...), custom_call_target="tpu_custom_call" | custom-call | tf_op jit(solution)/shard_map/back/pallas_call | solution.py:1190
  179.9 0.6 slice_bitcast_fusion.3
  180.5 0.6 slice_bitcast_fusion
  181.1 0.7 copy.39
  181.7 0.6 copy.40
  182.4 0.6 copy.41
  183.0 0.6 copy.42
  183.6 0.6 copy.43
  184.2 0.6 copy.44
  184.8 0.6 copy.45
  185.4 0.6 copy.46
  (1 shorter events, 0.0 us)
Async XLA Ops:
  5.1 0.9 copy-start.2
  6.0 59.3 %copy-start.4 = (bf16[1,128,640]{2,1,0:T(8,128)(2,1)S(1)}, bf16[1,128,640]{2,1,0:T(8,128)(2,1)}, u32[]{:S(2)}) copy-start(bf16[1,128,640]{2,1,0:T(8,128)(2,1)} %param.31) | copy-start | bytes 491524
  65.3 31.9 %copy-start.3 = (bf16[1,128,640]{2,1,0:T(8,128)(2,1)S(1)}, bf16[1,128,640]{2,1,0:T(8,128)(2,1)}, u32[]{:S(2)}) copy-start(bf16[1,128,640]{2,1,0:T(8,128)(2,1)} %param.16) | copy-start | bytes 491524
  93.2 1.9 %copy-start = (bf16[64,128,256]{2,1,0:T(8,128)(2,1)}, bf16[64,128,256]{2,1,0:T(8,128)(2,1)S(1)}, u32[]{:S(2)}) copy-start(bf16[64,128,256]{2,1,0:T(8,128)(2,1)S(1)} %get-tuple-element.57) | copy-start | bytes 12582916
  95.2 2.0 %copy-start.1 = (bf16[64,128,256]{2,1,0:T(8,128)(2,1)}, bf16[64,128,256]{2,1,0:T(8,128)(2,1)S(1)}, u32[]{:S(2)}) copy-start(bf16[64,128,256]{2,1,0:T(8,128)(2,1)S(1)} %get-tuple-element.58) | copy-start | bytes 12582916
